TPU v7x, 128 devices: a whole 4x4x4 slice. The times are simulated.
128 devices in a mesh: domain: 32 (over y, x, z_lo), inner: 4 (over z_hi, core).
Axes of the slice: x: 4, y: 4, z: 4 (z_hi: 2, z_lo: 2; z = z_hi * 2 + z_lo), core: 2. Of those that a mesh axis runs over, the one named last changes fastest.
Arguments:
- atom_cells: int32 [32, 4, 3, 512], P('domain', 'inner'), may hold values from 0 to 141, as said below
- atom_frac: float32 [32, 4, 3, 512], P('domain', 'inner'), may hold values from 0 to 1
- species: int32 [32, 4, 512], P('domain', 'inner'), may hold values from 0 to 7
- nbr_index: int32 [32, 4, 512, 32], P('domain', 'inner'), may hold values from 504 to 4103, as said below
- nbr_count: int32 [32, 4, 512], P('domain', 'inner'), may hold values from 4 to 32
- embed: bfloat16 [8, 128], replicated, may hold values from -6 to 6
- radial_in: bfloat16 [1, 8, 64], replicated, may hold values from -2 to 2
- radial_out: bfloat16 [1, 64, 384], replicated, may hold values from -0.75 to 0.75
- mix_weight: bfloat16 [1, 3, 128, 128], replicated, may hold values from -0.5 to 0.5
- product_weight: bfloat16 [1, 384, 128], replicated, may hold values from -0.3125 to 0.3125
- read_weight: bfloat16 [1, 128], replicated, may hold values from -0.5 to 0.5
- charge_weight: bfloat16 [128], replicated, may hold values from -0.5 to 0.5
Outputs:
- atom_energy: float32 [32, 4, 512], P('domain', 'inner')
- atom_potential: float32 [32, 4, 512], P('domain', 'inner')
Inputs may be any that keep to these rules, and one draw needn't show every extreme that they name: Within a block, atoms sit on a lattice of 4 x 16 x 8 sites 4 cells apart; component 0 of atom_cells is at most 13, component 1 at most 61, component 2 lies in 112 to 141. Two different atoms are at least 2 cells apart. `nbr_index`: each slot names an atom other than the atom itself, on a lattice site at most 2 sites away; live slots come first.
All inputs are finite; a program needn't handle non-finite values.
Results may differ from a plain program's by a relative error of at most 0.0059.
The roundings to bfloat16 on the way count: a program that leaves them out, or rounds other values in their place, can miss the bound.
Values may be sent and summed in bfloat16 or wider, within the bound.
A program may use at most 192 MiB of HBM per device.

v0:
```python
import math

import jax
import jax.numpy as jnp
from jax import lax
from jax.sharding import PartitionSpec as P

NB = 8
LX = 4
LY = 16
MZ = 256


spacing = 0.55
cutoff = 5.0
smearing = 0.2
coulomb = 14.399645
neighbour_scale = 0.25


def extended_2(cells, sides, width):
    for axis, dim in sides:
        count = lax.axis_size(axis)
        head = lax.slice_in_dim(cells, 0, width, axis=dim)
        tail = lax.slice_in_dim(cells, cells.shape[dim] - width, cells.shape[dim], axis=dim)
        cells = jnp.concatenate(
            [
                lax.ppermute(tail, axis, [(i, (i + 1) % count) for i in range(count)]),
                cells,
                lax.ppermute(head, axis, [((i + 1) % count, i) for i in range(count)]),
            ],
            axis=dim,
        )
    return cells


def from_behind(value, axis, steps):
    count = lax.axis_size(axis)
    pairs = [(source, (source + steps) % count) for source in range(count)]
    return lax.ppermute(value, axis, pairs)


def place_blocks(geo_ext, planes_x, planes_y):
    atom_count = geo_ext.shape[-1]
    steps_off = jnp.arange(3, dtype=jnp.float32) - 1.0
    off_x = jnp.broadcast_to(steps_off[:, None] * planes_x, (3, 3))
    off_y = jnp.broadcast_to(steps_off[None, :] * planes_y, (3, 3))
    offsets = jnp.stack([off_x, off_y, jnp.zeros((3, 3), jnp.float32)], axis=2)[..., None]
    placed = geo_ext + offsets
    return jnp.transpose(placed, (2, 0, 1, 3)).reshape(3, 9 * atom_count)


def edge_basis(placed, own_place, neighbours, live_count):
    atom_count, slot_count = neighbours.shape
    displacement = (placed[:, neighbours] - own_place[:, :, None]) * spacing
    distance = jnp.sqrt(jnp.sum(displacement * displacement, axis=0))
    direction = displacement / distance[None]
    scaled = distance / cutoff
    scaled_sq = scaled * scaled
    scaled_six = scaled_sq * scaled_sq * scaled_sq
    envelope = 1.0 - 28.0 * scaled_six + 48.0 * scaled_six * scaled - 21.0 * scaled_six * scaled_sq
    active = (jnp.arange(slot_count, dtype=jnp.int32)[None, :] < live_count[:, None]) & (
        scaled < 1.0
    )
    envelope = jnp.where(active, envelope, 0.0)
    bessel_order = jnp.arange(1, NB + 1, dtype=jnp.float32)
    radial_basis = (
        math.sqrt(2.0 / cutoff)
        * jnp.sin(bessel_order * (math.pi / cutoff) * distance[:, :, None])
        / distance[:, :, None]
    )
    along_x = direction[0]
    along_y = direction[1]
    along_z = direction[2]
    root_three = math.sqrt(3.0)
    root_fifteen = math.sqrt(15.0)
    root_five = math.sqrt(5.0)
    harmonic = jnp.stack(
        [
            jnp.ones_like(along_x),
            root_three * along_x,
            root_three * along_y,
            root_three * along_z,
            root_fifteen * along_x * along_y,
            root_fifteen * along_y * along_z,
            0.5 * root_five * (3.0 * along_z * along_z - 1.0),
            root_fifteen * along_x * along_z,
            0.5 * root_fifteen * (along_x * along_x - along_y * along_y),
        ],
        axis=-1,
    )
    return (radial_basis.astype(jnp.bfloat16), envelope, harmonic)


def message_layer(
    extended_state,
    node_state,
    radial_basis,
    envelope,
    harmonic,
    neighbours,
    weight_in,
    weight_out,
    weight_mix,
    weight_product,
    weight_read,
):
    atom_count, slot_count = neighbours.shape
    channels = node_state.shape[-1]
    hidden = jax.nn.silu(
        jnp.dot(
            radial_basis.reshape(atom_count * slot_count, -1),
            weight_in,
            preferred_element_type=jnp.float32,
        )
    ).astype(jnp.bfloat16)
    radial = (
        jnp.dot(hidden, weight_out, preferred_element_type=jnp.float32).reshape(
            atom_count, slot_count, 3, channels
        )
        * envelope[:, :, None, None]
    )
    neighbour_state = extended_state[neighbours]
    weighted = radial * neighbour_state[:, :, None, :].astype(jnp.float32)
    highest = lax.Precision.HIGHEST
    degree_zero = jnp.einsum("akc,ak->ac", weighted[:, :, 0], harmonic[:, :, 0], precision=highest)
    degree_one = jnp.einsum(
        "akc,akm->amc", weighted[:, :, 1], harmonic[:, :, 1:4], precision=highest
    )
    degree_two = jnp.einsum(
        "akc,akm->amc", weighted[:, :, 2], harmonic[:, :, 4:9], precision=highest
    )
    gathered = (
        jnp.concatenate([degree_zero[:, None], degree_one, degree_two], axis=1) * neighbour_scale
    ).astype(jnp.bfloat16)
    mixed_zero = jnp.dot(gathered[:, 0], weight_mix[0], preferred_element_type=jnp.float32)
    mixed_one = jnp.dot(
        gathered[:, 1:4].reshape(-1, channels), weight_mix[1], preferred_element_type=jnp.float32
    ).reshape(atom_count, 3, channels)
    mixed_two = jnp.dot(
        gathered[:, 4:9].reshape(-1, channels), weight_mix[2], preferred_element_type=jnp.float32
    ).reshape(atom_count, 5, channels)
    invariants = jnp.concatenate(
        [
            mixed_zero,
            jnp.sum(mixed_one * mixed_one, axis=1),
            jnp.sum(mixed_two * mixed_two, axis=1),
        ],
        axis=-1,
    ).astype(jnp.bfloat16)
    update = jax.nn.silu(jnp.dot(invariants, weight_product, preferred_element_type=jnp.float32))
    new_state = (node_state.astype(jnp.float32) + update).astype(jnp.bfloat16)
    energy_term = jnp.dot(new_state, weight_read, preferred_element_type=jnp.float32)
    return (new_state, energy_term)


def spline_weights(fraction):
    rest = 1.0 - fraction
    cube = fraction * fraction * fraction
    square = fraction * fraction
    return jnp.stack(
        [
            rest * rest * rest / 6.0,
            (3.0 * cube - 6.0 * square + 4.0) / 6.0,
            (-3.0 * cube + 3.0 * square + 3.0 * fraction + 1.0) / 6.0,
            cube / 6.0,
        ]
    )


def influence(freq_z, freq_x, freq_y, size_x, size_y, size_z):

    def signed_freq(wavenumber, length):
        return jnp.where(wavenumber < length // 2, wavenumber, wavenumber - length).astype(
            jnp.float32
        ) / (length * spacing)

    def modulus(wavenumber, length):
        cosine = jnp.cos(2.0 * math.pi / length * wavenumber.astype(jnp.float32))
        return (2.0 + cosine) * (2.0 + cosine) / 9.0

    along_z = signed_freq(freq_z, size_z)[:, None, None]
    along_x = signed_freq(freq_x, size_x)[None, :, None]
    along_y = signed_freq(freq_y, size_y)[None, None, :]
    squared = along_z * along_z + along_x * along_x + along_y * along_y
    safe_sq = jnp.where(squared > 0.0, squared, 1.0)
    moduli = (
        modulus(freq_z, size_z)[:, None, None]
        * modulus(freq_x, size_x)[None, :, None]
        * modulus(freq_y, size_y)[None, None, :]
    )
    volume = size_x * size_y * size_z * spacing * spacing * spacing
    values = (
        coulomb
        * jnp.exp(-2.0 * math.pi * math.pi * smearing * smearing * squared)
        / (math.pi * volume * safe_sq * moduli)
    )
    return jnp.where(squared > 0.0, values, 0.0)


def stencil(cell_index, weights, first_cell, cell_span):
    grid_cells = jnp.arange(cell_span, dtype=jnp.int32) + first_cell
    summed = jnp.zeros((cell_index.shape[0], cell_span), jnp.float32)
    for offset in range(4):
        summed = summed + weights[offset][:, None] * (
            grid_cells[None, :] == (cell_index + offset - 1)[:, None]
        ).astype(jnp.float32)
    return summed


def spread(charge, sten_x, sten_y, sten_z):
    atom_count = sten_x.shape[0]
    left_part = (charge[:, None, None] * sten_x[:, :, None] * sten_y[:, None, :]).reshape(
        atom_count, -1
    )
    product = jnp.einsum("ap,az->pz", left_part, sten_z, precision=lax.Precision.HIGHEST)
    return product.reshape(sten_x.shape[1], sten_y.shape[1], sten_z.shape[1])


def interpolate(widened, sten_x, sten_y, sten_z):
    atom_count = sten_x.shape[0]
    profile = jnp.einsum(
        "pz,az->pa", widened.reshape(-1, widened.shape[-1]), sten_z, precision=lax.Precision.HIGHEST
    )
    outer_weight = (sten_x[:, :, None] * sten_y[:, None, :]).reshape(atom_count, -1)
    return jnp.einsum("pa,ap->a", profile, outer_weight, precision=lax.Precision.HIGHEST)


def tables(length):
    serial = jnp.arange(length, dtype=jnp.int32)
    product = serial[:, None] * serial[None, :] % length
    angles = product.astype(jnp.float32) * (2.0 * math.pi / length)
    return (jnp.cos(angles), jnp.sin(angles))


def transform(spectrum, cos_table, sin_table, einsum_form, direction_sign):
    highest = lax.Precision.HIGHEST
    real_cos = jnp.einsum(einsum_form, spectrum[0], cos_table, precision=highest)
    real_sin = jnp.einsum(einsum_form, spectrum[0], sin_table, precision=highest)
    imag_cos = jnp.einsum(einsum_form, spectrum[1], cos_table, precision=highest)
    imag_sin = jnp.einsum(einsum_form, spectrum[1], sin_table, precision=highest)
    return jnp.stack([real_cos - direction_sign * imag_sin, imag_cos + direction_sign * real_sin])


def send_inner(spectrum):
    return lax.all_to_all(spectrum, "inner", split_axis=1, concat_axis=3, tiled=True)


def send_domain(spectrum):
    return lax.all_to_all(spectrum, "domain", split_axis=1, concat_axis=2, tiled=True)


def back_domain(spectrum):
    return lax.all_to_all(
        spectrum.astype(jnp.bfloat16), "domain", split_axis=2, concat_axis=1, tiled=True
    ).astype(spectrum.dtype)


def back_inner(spectrum):
    return lax.all_to_all(
        spectrum.astype(jnp.bfloat16), "inner", split_axis=3, concat_axis=1, tiled=True
    ).astype(spectrum.dtype)


def local(
    atom_cells,
    atom_frac,
    species,
    nbr_index,
    nbr_count,
    embed,
    radial_in,
    radial_out,
    mix_weight,
    product_weight,
    read_weight,
    charge_weight,
):
    atom_count = species.shape[-1]
    channels = embed.shape[1]
    domain_count = lax.axis_size("domain")
    inner_count = lax.axis_size("inner")
    planes_x = 4 * LX
    planes_y = 4 * LY
    depth = MZ
    full_x = planes_x * domain_count
    full_y = planes_y * inner_count
    plane_first = 0
    geometry = atom_cells.astype(jnp.float32) + atom_frac
    geo_ext = extended_2(geometry, (("domain", 0), ("inner", 1)), 1)
    placed = place_blocks(geo_ext, planes_x, planes_y)
    neighbours = nbr_index[0, 0]
    radial_basis, envelope, harmonic = edge_basis(
        placed, geometry[0, 0], neighbours, nbr_count[0, 0]
    )
    species_onehot = (
        species[0, 0][:, None] == jnp.arange(embed.shape[0], dtype=jnp.int32)[None, :]
    ).astype(jnp.bfloat16)
    node_state = jnp.dot(species_onehot, embed, preferred_element_type=jnp.float32).astype(
        jnp.bfloat16
    )
    extended = extended_2(node_state[None, None], (("domain", 0), ("inner", 1)), 1)
    node_state, energy_term = message_layer(
        extended.reshape(9 * atom_count, channels),
        node_state,
        radial_basis,
        envelope,
        harmonic,
        neighbours,
        radial_in[0],
        radial_out[0],
        mix_weight[0],
        product_weight[0],
        read_weight[0],
    )
    latent = jnp.dot(node_state, charge_weight, preferred_element_type=jnp.float32)
    summed = lax.psum(jnp.sum(latent), ("domain", "inner"))
    charge = latent - summed / (atom_count * domain_count * inner_count)
    cell_index = atom_cells[0, 0]
    weights = spline_weights(atom_frac[0, 0])
    sten_x = stencil(cell_index[0], weights[:, 0], -1, planes_x + 1)
    sten_y = stencil(cell_index[1], weights[:, 1], -1, planes_y + 1)
    sten_z = stencil(cell_index[2], weights[:, 2], plane_first, depth)
    charge_mesh = spread(charge, sten_x, sten_y, sten_z)
    arrived = from_behind(charge_mesh[0].astype(jnp.bfloat16), "domain", -1).astype(jnp.float32)
    charge_mesh = charge_mesh[1:].at[planes_x - 1].add(arrived)
    arrived = from_behind(charge_mesh[:, 0].astype(jnp.bfloat16), "inner", -1).astype(jnp.float32)
    charge_mesh = charge_mesh[:, 1:].at[:, planes_y - 1].add(arrived)
    cos_y, sin_y = tables(full_y)
    cos_x, sin_x = tables(full_x)
    highest = lax.Precision.HIGHEST
    domain_at = lax.axis_index("domain")
    inner_at = lax.axis_index("inner")
    cos_z, sin_z = tables(depth)
    real_part = jnp.einsum("xyz,zk->kxy", charge_mesh, cos_z, precision=highest)
    imag_part = -jnp.einsum("xyz,zk->kxy", charge_mesh, sin_z, precision=highest)
    spectrum = jnp.stack([real_part, imag_part])
    spectrum = send_inner(spectrum)
    spectrum = transform(spectrum, cos_y, sin_y, "zxy,yk->zxk", -1.0)
    spectrum = send_domain(spectrum)
    spectrum = transform(spectrum, cos_x, sin_x, "zxy,xk->zky", -1.0)
    kz_first = inner_at * (depth // inner_count) + domain_at * (
        depth // (inner_count * domain_count)
    )
    kz_values = kz_first + jnp.arange(spectrum.shape[1], dtype=jnp.int32)
    influence_mesh = influence(
        kz_values,
        jnp.arange(full_x, dtype=jnp.int32),
        jnp.arange(full_y, dtype=jnp.int32),
        full_x,
        full_y,
        depth,
    )
    spectrum = spectrum * influence_mesh[None]
    spectrum = transform(spectrum, cos_x, sin_x, "zxy,xk->zky", 1.0)
    spectrum = back_domain(spectrum)
    spectrum = transform(spectrum, cos_y, sin_y, "zxy,yk->zxk", 1.0)
    spectrum = back_inner(spectrum)
    potential = jnp.einsum("kxy,kz->xyz", spectrum[0], cos_z, precision=highest) - jnp.einsum(
        "kxy,kz->xyz", spectrum[1], sin_z, precision=highest
    )
    plane_rim = from_behind(potential[planes_x - 1].astype(jnp.bfloat16), "domain", 1).astype(
        jnp.float32
    )
    widened = jnp.concatenate([plane_rim[None], potential], axis=0)
    row_rim = from_behind(widened[:, planes_y - 1], "inner", 1)
    widened = jnp.concatenate([row_rim[:, None], widened], axis=1)
    potential_at = interpolate(widened, sten_x, sten_y, sten_z)
    atom_energy = energy_term + 0.5 * charge * potential_at
    return (atom_energy[None, None], potential_at[None, None])


def solution(mesh):
    in_specs = (
        P("domain", "inner", None, None),
        P("domain", "inner", None, None),
        P("domain", "inner", None),
        P("domain", "inner", None, None),
        P("domain", "inner", None),
        P(),
        P(),
        P(),
        P(),
        P(),
        P(),
        P(),
    )
    out_specs = (P("domain", "inner", None), P("domain", "inner", None))
    return jax.shard_map(local, mesh=mesh, in_specs=in_specs, out_specs=out_specs, check_vma=False)
```

profile of v0, /device:TPU:1, one launch (start us, length us, event | category | flops | bytes accessed | tf_op | source)
XLA Modules:
  0.0 607.5 jit_solution(15236328566828327901)
XLA Ops:
  1.4 2.5 collective-permute-start
  3.9 4.7 collective-permute-start.1
  9.7 5.7 collective-permute-start.5
  20.2 4.8 collective-permute-start.2
  25.9 3.8 collective-permute-done.3
  30.4 54.8 %gather_fusion = f32[16384,3]{1,0:T(8,128)} fusion(f32[3,4608]{0,1:T(8,128)S(1)} %bitcast.315, s32[16384]{0:T(1024)S(1)} %broadcast_clamp_fusion), kind=kCustom, calls=%fused_computation | custom fusion | bytes 458752 | tf_op jit(solution)/shard_map/gather | solution.py:55
  85.2 5.3 copy.216
  92.9 3.0 multiply_convert_fusion
  99.4 3.1 copy.218
  108.2 57.9 %gather_fusion.1 = bf16[16384,128]{1,0:T(8,128)(2,1)} fusion(bf16[4608,128]{1,0:T(8,128)(2,1)S(1)} %bitcast.314, s32[16384]{0:T(1024)S(1)} %broadcast_clamp_fusion), kind=kCustom, calls=%fused_computation.1 | custom fusion | bytes 8454144 | tf_op jit(solution)/shard_map/gather | solution.py:123
  166.1 6.9 %copy.221 = f32[512,32,128]{2,0,1:T(8,128)} copy(bf16[512,32,128]{2,1,0:T(8,128)(2,1)} %bitcast.316) | data formatting | bytes 12582912 | tf_op jit(solution)/shard_map/convert_element_type | solution.py:124
  173.0 13.0 %multiply_multiply_fusion = f32[512,32,3,128]{3,0,2,1:T(8,128)} fusion(f32[512,32,128]{2,0,1:T(8,128)} %copy.221, f32[512,32]{0,1:T(8,128)S(1)} %get-tuple-element.42, bf16[512,32,64,1]{2,1,0,3:T(8,128)(2,1)S(1)} %bitcast.317, bf16[1,64,384]{2,1,0:T(8,128)(2,1)S(1)} %copy-done.18), kind=kOutput, calls=%fused_computation.2 | convolution fusion | flops 817889280 | bytes 35766272 | tf_op jit(solution)/shard_map/dot_general | solution.py:118
  186.0 17.5 %slice_bitcast_fusion.2 = (f32[512,32,128]{2,0,1:T(8,128)}, f32[512,32,128]{2,0,1:T(8,128)}, f32[512,32,128]{2,0,1:T(8,128)}) fusion(f32[512,32,3,128]{3,0,2,1:T(8,128)} %multiply_multiply_fusion), kind=kLoop, calls=%fused_computation.5 | loop fusion | bytes 50331648 | tf_op jit(solution)/shard_map/squeeze | solution.py:126
  203.6 15.3 %fusion = f32[512,1,128]{2,1,0:T(1,128)S(1)} fusion(f32[512,32,128]{2,0,1:T(8,128)} %get-tuple-element.26), kind=kOutput, calls=%fused_computation.6 | convolution fusion | flops 25165824 | bytes 8650752 | tf_op jit(solution)/shard_map/akc,ak->ac/dot_general | solution.py:126
  218.9 11.2 %fusion.4 = f32[512,3,128]{2,1,0:T(4,128)S(1)} fusion(f32[512,32,3]{1,2,0:T(4,128)S(1)} %copy-done.10, f32[512,32,128]{2,0,1:T(8,128)S(1)} %copy-done.2), kind=kOutput, calls=%fused_computation.10 | convolution fusion | flops 75497472 | bytes 9371648 | tf_op jit(solution)/shard_map/akc,akm->amc/dot_general | solution.py:127
  230.1 11.7 %fusion.2 = f32[512,5,128]{2,1,0:T(8,128)S(1)} fusion(f32[512,32,5]{1,2,0:T(8,128)S(1)} %copy.224, f32[512,32,128]{2,0,1:T(8,128)S(1)} %copy-done.3), kind=kOutput, calls=%fused_computation.8 | convolution fusion | flops 125829120 | bytes 10027008 | tf_op jit(solution)/shard_map/akc,akm->amc/dot_general | solution.py:130
  246.5 63.0 %psum.7 = f32[]{:T(128)} all-reduce(f32[]{:T(128)} %reduce_sum.39), channel_id=1, replica_groups=mesh['domain'=32,'inner'=4] {'domain','inner'}, use_global_device_ids=true, to_apply=%region_4.5 | all-reduce | flops 1 | bytes 8 | tf_op jit(solution)/shard_map/psum | solution.py:317
  310.3 2.1 broadcast_multiply_fusion.1
  312.4 3.2 mul.1061
  315.6 3.9 fusion.64
  319.6 3.0 collective-permute-start.8
  323.7 2.4 slice.276
  329.8 2.4 slice.322
  335.8 3.3 convolution_bitcast_fusion.1
  339.1 2.0 fusion.14
  342.6 5.6 copy.230
  348.2 5.5 reshape.1284
  353.7 30.5 %all_to_all.60 = f32[4,1,131072]{2,1,0:T(1,128)} all-to-all(f32[4,1,131072]{2,1,0:T(1,128)} %reshape.1284), channel_id=1, replica_groups=mesh['domain'=32,'inner'=4] {'inner'}, dimensions={0} | all-to-all | bytes 4194304 | tf_op jit(solution)/shard_map/all_to_all | solution.py:246
  384.7 9.1 %reduce.6 = f32[4,131072]{1,0:T(4,128)} reduce(f32[4,1,131072]{2,1,0:T(1,128)} %all_to_all.60, f32[]{:T(128)} %broadcast.1254), dimensions={1}, to_apply=%all_to_all.44.reduce_sub_computation | reduce | bytes 4194308 | tf_op jit(solution)/shard_map/all_to_all | solution.py:246
  393.8 5.5 reshape.1285
  399.4 4.9 copy.284
  404.2 2.4 fusion.267
  406.6 3.4 squeeze.122
  410.0 4.2 fusion.89
  414.1 3.2 squeeze.123
  417.4 3.3 fusion.87
  420.7 2.0 fusion.18
  422.8 2.0 fusion.16
  426.4 5.9 all-to-all-start.1
  434.2 25.7 %all-to-all-done.1 = f32[2,64,16,256]{3,2,0,1:T(8,128)} async-done(((f32[2,64,16,256]{3,2,0,1:T(8,128)}), f32[2,64,16,256]{3,2,0,1:T(8,128)}, u32[]{:S(2)}, u32[]{:S(2)}) %all-to-all-start.1) | async-done | bytes 2097184 | tf_op jit(solution)/shard_map/all_to_all | solution.py:250
  459.9 1.8 copy.286
  461.9 5.7 fusion.48
  467.6 6.1 %fusion.46 = f32[512,2,256]{2,0,1:T(8,128)S(1)} fusion(f32[2,512,256]{2,1,0:T(8,128)S(1)} %bitcast.338), kind=kOutput, calls=%fused_computation.90 | convolution fusion | flops 1614282752 | bytes 2097152 | tf_op jit(solution)/shard_map/zxy,xk->zky/dot_general | solution.py:240
  473.7 5.7 fusion.13
  479.4 5.7 fusion.11
  485.4 5.9 fusion.44
  491.3 5.7 fusion.42
  497.0 5.9 fusion.27
  502.9 5.7 fusion.26
  509.8 21.0 %all_to_all.61 = bf16[2,2,512,256]{3,1,0,2:T(2,128)(2,1)S(1)} all-to-all(bf16[2,2,512,256]{3,1,0,2:T(2,128)(2,1)S(1)} %copy.234), channel_id=1, replica_groups=mesh['domain'=32,'inner'=4] {'domain'}, dimensions={2} | all-to-all | bytes 2097152 | tf_op jit(solution)/shard_map/all_to_all | solution.py:254
  538.6 5.3 copy.236
  543.9 4.4 reshape.1286
  548.3 22.2 %all_to_all.62 = bf16[4,2,65536]{2,1,0:T(2,128)(2,1)} all-to-all(bf16[4,2,65536]{2,1,0:T(2,128)(2,1)} %reshape.1286), channel_id=1, replica_groups=mesh['domain'=32,'inner'=4] {'inner'}, dimensions={0} | all-to-all | bytes 2097152 | tf_op jit(solution)/shard_map/all_to_all | solution.py:260
  570.5 4.3 reshape.1287
  574.8 3.2 copy.285
  578.0 2.3 fusion.268
  580.2 2.1 squeeze.130
  582.3 2.6 fusion.81
  584.9 2.1 squeeze.131
  587.0 2.8 convolution_subtract_fusion
  589.9 7.0 %collective-permute-done.10 = bf16[64,256]{1,0:T(8,128)(2,1)S(1)} collective-permute-done((bf16[64,256]{1,0:T(8,128)(2,1)S(1)}, bf16[64,256]{1,0:T(8,128)(2,1)S(1)}, u32[]{:S(2)}, u32[]{:S(2)}) %collective-permute-start.10) | collective-permute-done | bytes 32800 | tf_op jit(solution)/shard_map/ppermute | solution.py:40
  596.9 2.2 collective-permute-start.11
  599.3 1.8 mul.1108
  602.6 4.1 fusion.9
  (170 shorter events, 49.8 us)
Async XLA Ops:
  0.6 244.7 %copy-start = (bf16[1,384,128]{2,1,0:T(8,128)(2,1)S(1)}, bf16[1,384,128]{2,1,0:T(8,128)(2,1)}, u32[]{:S(2)}) copy-start(bf16[1,384,128]{2,1,0:T(8,128)(2,1)} %param.25) | copy-start | bytes 294916
  1.4 18.8 %collective-permute-start = (f32[1,1,3,512]{3,1,2,0:T(1,128)S(1)}, f32[1,1,3,512]{3,1,2,0:T(1,128)S(1)}, u32[]{:S(2)}, u32[]{:S(2)}) collective-permute-start(f32[1,1,3,512]{3,1,2,0:T(1,128)S(1)} %convert_add_fusion), channel_id=1, source_target_pairs={{0,4},{4,8},{8,12},{12,16},{16,20},{20,24},{24,28},{28,32},{32,36}... | collective-permute-start | bytes 18440 | tf_op jit(solution)/shard_map/ppermute | solution.py:28
  3.9 16.2 %collective-permute-start.1 = (f32[1,1,3,512]{3,1,2,0:T(1,128)S(1)}, f32[1,1,3,512]{3,1,2,0:T(1,128)S(1)}, u32[]{:S(2)}, u32[]{:S(2)}) collective-permute-start(f32[1,1,3,512]{3,1,2,0:T(1,128)S(1)} %convert_add_fusion), channel_id=1, source_target_pairs={{4,0},{8,4},{12,8},{16,12},{20,16},{24,20},{28,24},{32,28},{36,32}... | collective-permute-start | bytes 18440 | tf_op jit(solution)/shard_map/ppermute | solution.py:30
  9.6 87.0 %copy-start.13 = (bf16[512,128]{1,0:T(8,128)(2,1)}, bf16[512,128]{1,0:T(8,128)(2,1)S(1)}, u32[]{:S(2)}) copy-start(bf16[512,128]{1,0:T(8,128)(2,1)S(1)} %convolution_convert_fusion) | copy-start | bytes 393220
  9.6 87.0 %collective-permute-start.4 = (bf16[1,1,512,128]{3,2,1,0:T(8,128)(2,1)S(1)}, bf16[1,1,512,128]{3,2,1,0:T(8,128)(2,1)S(1)}, u32[]{:S(2)}, u32[]{:S(2)}) collective-permute-start(bf16[1,1,512,128]{3,2,1,0:T(8,128)(2,1)S(1)} %bitcast.332), channel_id=1, source_target_pairs={{0,4},{4,8},{8,12},{12,16},{16,20},{20,24},{24,28},{28,32},{32,36}... | collective-permute-start | bytes 393224 | tf_op jit(solution)/shard_map/ppermute | solution.py:28
  9.7 86.9 %collective-permute-start.5 = (bf16[1,1,512,128]{3,2,1,0:T(8,128)(2,1)S(1)}, bf16[1,1,512,128]{3,2,1,0:T(8,128)(2,1)S(1)}, u32[]{:S(2)}, u32[]{:S(2)}) collective-permute-start(bf16[1,1,512,128]{3,2,1,0:T(8,128)(2,1)S(1)} %bitcast.333), channel_id=1, source_target_pairs={{4,0},{8,4},{12,8},{16,12},{20,16},{24,20},{28,24},{32,28},{36,32}... | collective-permute-start | bytes 393224 | tf_op jit(solution)/shard_map/ppermute | solution.py:30
  20.2 5.7 collective-permute-start.2
  25.0 4.7 collective-permute-start.3
  85.2 5.3 copy-start.24
  90.5 2.4 copy-start.28
  96.6 6.0 copy-start.16
  96.6 6.0 copy-start.17
  97.4 8.5 %collective-permute-start.6 = (bf16[3,1,512,128]{3,2,1,0:T(8,128)(2,1)}, bf16[3,1,512,128]{3,2,1,0:T(8,128)(2,1)}, u32[]{:S(2)}, u32[]{:S(2)}) collective-permute-start(bf16[3,1,512,128]{3,2,1,0:T(8,128)(2,1)} %pad_maximum_fusion.5), channel_id=1, source_target_pairs={{0,1},{1,2},{2,3},{3,0},{4,5},{5,6},{6,7},{7,4},{8,9},{9,10},{10,1... | collective-permute-start | bytes 1179656 | tf_op jit(solution)/shard_map/ppermute | solution.py:28
  97.5 9.4 %collective-permute-start.7 = (bf16[3,1,512,128]{3,2,1,0:T(8,128)(2,1)}, bf16[3,1,512,128]{3,2,1,0:T(8,128)(2,1)}, u32[]{:S(2)}, u32[]{:S(2)}) collective-permute-start(bf16[3,1,512,128]{3,2,1,0:T(8,128)(2,1)} %pad_maximum_fusion.5), channel_id=1, source_target_pairs={{1,0},{2,1},{3,2},{0,3},{5,4},{6,5},{7,6},{4,7},{9,8},{10,9},{11,1... | collective-permute-start | bytes 1179656 | tf_op jit(solution)/shard_map/ppermute | solution.py:30
  166.1 6.9 %copy-start.4 = (bf16[16384,64]{1,0:T(8,128)(2,1)S(1)}, bf16[16384,64]{1,0:T(8,128)(2,1)}, u32[]{:S(2)}) copy-start(bf16[16384,64]{1,0:T(8,128)(2,1)} %copy.218) | copy-start | bytes 6291460
  166.1 6.9 %copy-start.18 = (bf16[1,64,384]{2,1,0:T(8,128)(2,1)S(1)}, bf16[1,64,384]{2,1,0:T(8,128)(2,1)}, u32[]{:S(2)}) copy-start(bf16[1,64,384]{2,1,0:T(8,128)(2,1)} %param.23) | copy-start | bytes 147460
  186.0 32.9 %copy-start.10 = (f32[512,32,3]{1,2,0:T(4,128)S(1)}, f32[512,32,3]{1,2,0:T(4,128)}, u32[]{:S(2)}) copy-start(f32[512,32,3]{1,2,0:T(4,128)} %copy.222) | copy-start | bytes 589828
  203.6 15.3 %copy-start.2 = (f32[512,32,128]{2,0,1:T(8,128)S(1)}, f32[512,32,128]{2,0,1:T(8,128)}, u32[]{:S(2)}) copy-start(f32[512,32,128]{2,0,1:T(8,128)} %get-tuple-element.28) | copy-start | bytes 25165828
  218.9 11.2 %copy-start.3 = (f32[512,32,128]{2,0,1:T(8,128)S(1)}, f32[512,32,128]{2,0,1:T(8,128)}, u32[]{:S(2)}) copy-start(f32[512,32,128]{2,0,1:T(8,128)} %get-tuple-element.27) | copy-start | bytes 25165828
  243.3 0.9 copy-start.19
  243.7 1.6 copy-start.14
  244.5 1.1 copy-start.26
  244.7 65.6 %copy-start.15 = (f32[512,65]{0,1:T(8,128)S(1)}, f32[512,65]{0,1:T(8,128)}, u32[]{:S(2)}) copy-start(f32[512,65]{0,1:T(8,128)} %select_add_fusion.3) | copy-start | bytes 399364
  312.4 3.2 copy-start.20
  312.4 3.2 copy-start.21
  312.4 3.2 copy-start.22
  312.4 3.2 copy-start.23
  319.6 3.1 copy-start.9
  319.6 6.5 %collective-permute-start.8 = (bf16[65,256]{1,0:T(8,128)(2,1)S(1)}, bf16[65,256]{1,0:T(8,128)(2,1)S(1)}, u32[]{:S(2)}, u32[]{:S(2)}) collective-permute-start(bf16[65,256]{1,0:T(8,128)(2,1)S(1)} %slice.390), channel_id=1, source_target_pairs={{0,124},{4,0},{8,4},{12,8},{16,12},{20,16},{24,20},{28,24},{32,28}... | collective-permute-start | bytes 99848 | tf_op jit(solution)/shard_map/ppermute | solution.py:40
  328.6 4.6 collective-permute-start.9
  335.8 3.3 copy-start.8
  417.4 3.3 copy-start.7
  417.4 3.4 copy-start.12
  420.7 2.0 copy-start.6
  426.4 33.5 %all-to-all-start.1 = ((f32[2,64,16,256]{3,2,0,1:T(8,128)}), f32[2,64,16,256]{3,2,0,1:T(8,128)}, u32[]{:S(2)}, u32[]{:S(2)}) async-start(f32[2,64,16,256]{3,2,0,1:T(8,128)} %copy.232), calls=%async_computation.1 | async-start | bytes 4194304 | tf_op jit(solution)/shard_map/all_to_all | solution.py:250
  479.4 5.7 copy-start.11
  587.0 12.2 %copy-start.27 = (bf16[1,128]{1,0:T(2,128)(2,1)S(1)}, bf16[1,128]{1,0:T(2,128)(2,1)}, u32[]{:S(2)}) copy-start(bf16[1,128]{1,0:T(2,128)(2,1)} %param.26) | copy-start | bytes 772
  589.8 7.1 %copy-start.5 = (f32[16,64,256]{2,1,0:T(8,128)}, f32[16,64,256]{2,1,0:T(8,128)S(1)}, u32[]{:S(2)}) copy-start(f32[16,64,256]{2,1,0:T(8,128)S(1)} %convolution_subtract_fusion) | copy-start | bytes 3145732
  589.8 7.1 %collective-permute-start.10 = (bf16[64,256]{1,0:T(8,128)(2,1)S(1)}, bf16[64,256]{1,0:T(8,128)(2,1)S(1)}, u32[]{:S(2)}, u32[]{:S(2)}) collective-permute-start(bf16[64,256]{1,0:T(8,128)(2,1)S(1)} %fusion.155), channel_id=1, source_target_pairs={{0,4},{4,8},{8,12},{12,16},{16,20},{20,24},{24,28},{28,32},{32,36}... | collective-permute-start | bytes 98312 | tf_op jit(solution)/shard_map/ppermute | solution.py:40
  596.9 4.1 collective-permute-start.11
  602.4 4.9 copy-start.1
  606.7 0.6 copy-start.25
where the time goes:
time: 616 us; the launch traced here: 608 us
  local copies, waits for them, and re-layouts  225 us (37%)
  matrix products  140 us (23%)
  blocking collectives  137 us (22%)
  waiting for transfers between devices  40.3 us (7%)
  other arithmetic  32.3 us (5%)
  starting transfers between devices  30.9 us (5%)
    psum x1, blocking collectives, local(): summed = lax.psum(jnp.sum(latent), ('domain', 'inner'))  63 us
    gather x2, local copies, waits for them, and re-layouts, edge_basis(): displacement = (placed[:, neighbours] - own_place[:, :, None]) * spacing  60 us
    gather x1, local copies, waits for them, and re-layouts, message_layer(): neighbour_state = extended_state[neighbours]  57.9 us
    all_to_all x1, blocking collectives, send_inner(): lax.all_to_all(spectrum, 'inner', split_axis=1, concat_axis=3, tiled=True)  30.5 us
    all_to_all x1, waiting for transfers between devices, send_domain(): lax.all_to_all(spectrum, 'domain', split_axis=1, concat_axis=2, tiled=True)  25.7 us
    all_to_all x1, blocking collectives, back_inner(): lax.all_to_all(spectrum.astype(jnp.bfloat16), 'inner', split_axis=3, conc...  22.2 us
    all_to_all x1, blocking collectives, back_domain(): lax.all_to_all(spectrum.astype(jnp.bfloat16), 'domain', split_axis=2, con...  21 us
    unnamed x65, local copies, waits for them, and re-layouts  19.9 us
  transfers between devices with their start and end apart: 13, of which 7 were waited for; matrix products, arithmetic and copies ran while one was open for 15% of the time, Pallas kernels for 0%

commit v1 on v0

v1 whole, which is shorter than its diff:
```python
import functools
import math

import jax
import jax.numpy as jnp
import ml_dtypes
import numpy as np
from jax import lax
from jax.experimental import pallas as pl
from jax.experimental.pallas import tpu as pltpu
from jax.sharding import PartitionSpec as P

MESH = pl.DeviceIdType.MESH
VMEM = pltpu.VMEM
F32 = jnp.float32
BF16 = jnp.bfloat16

spacing = 0.55
cutoff = 5.0
smearing = 0.2
coulomb = 14.399645
neighbour_scale = 0.25

Z_LOW = 111
Z_SPAN = 33
PLANES = 2 * Z_SPAN
ROW_LOW = 504 // 128
ROW_HIGH = 4103 // 128

DEGREE = (0, 1, 1, 1, 2, 2, 2, 2, 2)


def dot(a, b):
    return lax.dot_general(a, b, (((1,), (0,)), ((), ())), preferred_element_type=F32)


def dot_nt(a, b):
    return lax.dot_general(a, b, (((1,), (1,)), ((), ())), preferred_element_type=F32)


def split(x):
    high = x.astype(BF16)
    return high, (x - high.astype(F32)).astype(BF16)


def dot_split(a, b, form):
    return form(a[0], b[0]) + (form(a[0], b[1]) + form(a[1], b[0]))


def basis_rows(length, positions):
    half = length // 2
    k = np.arange(half)
    angle = 2.0 * np.pi * ((k[:, None] * positions[None, :]) % length) / length
    cosine = np.cos(angle)
    sine = np.sin(angle)
    sine[0] = np.cos(np.pi * positions)
    return np.concatenate([cosine, sine], axis=0)


def host_split(x):
    x = x.astype(np.float32)
    high = x.astype(ml_dtypes.bfloat16)
    low = (x - high.astype(np.float32)).astype(ml_dtypes.bfloat16)
    return high, low


@functools.lru_cache(maxsize=None)
def host_tables(domain_count, inner_count, planes_x, planes_y, depth):
    full_x = planes_x * domain_count
    full_y = planes_y * inner_count
    table_x = basis_rows(full_x, np.arange(full_x))
    table_y = np.zeros((inner_count, 128, 3, full_y))
    for i in range(inner_count):
        all_y = basis_rows(full_y, (planes_y * i - 1 + np.arange(planes_y + 1)) % full_y).T
        table_y[i, : planes_y + 1, 0] = all_y
        table_y[i, 65:98, 1] = all_y[:33]
        table_y[i, 65:97, 2] = all_y[33:]
    table_y = table_y.reshape(inner_count * 128, 3 * full_y)

    def squared_freq(length, count):
        return (np.arange(count) / (length * spacing)) ** 2

    def modulus(length, count):
        return (2.0 + np.cos(2.0 * np.pi * np.arange(count) / length)) ** 2 / 9.0

    def twice(length, count):
        k = np.arange(count)
        return np.where((k == 0) | (k == length // 2), 1.0, 2.0)

    cx, cy, cz = full_x // 2 + 1, full_y // 2 + 1, depth // 2 + 1
    squared = (
        squared_freq(full_x, cx)[:, None, None]
        + squared_freq(full_y, cy)[None, :, None]
        + squared_freq(depth, cz)[None, None, :]
    )
    safe = np.where(squared > 0.0, squared, 1.0)
    moduli = (
        modulus(full_x, cx)[:, None, None]
        * modulus(full_y, cy)[None, :, None]
        * modulus(depth, cz)[None, None, :]
    )
    volume = full_x * full_y * depth * spacing**3
    kernel = (
        coulomb
        * np.exp(-2.0 * np.pi**2 * smearing**2 * squared)
        / (np.pi * volume * safe * moduli)
    )
    kernel = np.where(squared > 0.0, kernel, 0.0)
    kernel = kernel * twice(full_x, cx)[:, None, None] * twice(full_y, cy)[None, :, None]
    step = np.arange(Z_SPAN)
    along = np.cos(2.0 * np.pi * np.arange(cz)[:, None] * step[None, :] / depth)
    along = along * twice(depth, cz)[:, None]
    wave = np.cos(np.pi * (2 * np.arange(Z_SPAN)[None, :] + 1) * step[:, None] / (2 * Z_SPAN))
    wave = wave * np.where(step == 0, 1.0, 2.0)[:, None] / Z_SPAN
    gain = np.moveaxis(kernel @ (along @ wave), 2, 0)
    order_y = np.concatenate([np.arange(full_y // 2), [full_y // 2], np.arange(1, full_y // 2)])
    gain = gain[:, :, order_y]
    half = full_x // 2
    padded = np.zeros((Z_SPAN, half + 8, full_y), np.float32)
    padded[:, :half] = gain[:, :half]
    padded[:, half] = gain[:, half]
    plane = np.arange(PLANES)
    angle = (
        np.pi * (2 * (plane // 2)[:, None] + 1) * np.arange(40)[None, :] / (2 * Z_SPAN)
    )
    zeta = np.where(plane[:, None] % 2 == 0, np.cos(angle), np.sin(angle))
    zeta[:, Z_SPAN:] = 0.0
    zeta_full = np.zeros((72, 40), np.float32)
    zeta_full[:PLANES] = zeta
    return dict(
        x=host_split(table_x),
        xt=host_split(table_x.T),
        y=host_split(table_y),
        gain=padded,
        zeta=zeta_full,
    )


def exchange_kernel(counts, cells_ref, frac_ref, species_ref, ext_ref, mine, send_sem, recv_sem):
    at = (lax.axis_index("domain"), lax.axis_index("inner"))
    barrier = pltpu.get_barrier_semaphore()
    moves = [(dx, dy) for dx in (-1, 0, 1) for dy in (-1, 0, 1) if (dx, dy) != (0, 0)]

    def target(move):
        return tuple(lax.rem(at[n] + counts[n] + move[n], counts[n]) for n in range(2))

    for move in moves:
        pl.semaphore_signal(barrier, inc=1, device_id=target(move), device_id_type=MESH)
    mine[...] = jnp.zeros_like(mine)
    mine[0:3, :] = cells_ref[...].astype(F32) + frac_ref[...]
    mine[3:4, :] = species_ref[...].astype(F32)
    pl.semaphore_wait(barrier, len(moves))
    copies = []
    for n, (dx, dy) in enumerate(moves):
        copy = pltpu.make_async_remote_copy(
            src_ref=mine,
            dst_ref=ext_ref.at[(1 - dx) * 3 + (1 - dy)],
            send_sem=send_sem.at[n],
            recv_sem=recv_sem.at[n],
            device_id=target((dx, dy)),
            device_id_type=MESH,
        )
        copy.start()
        copies.append(copy)
    ext_ref[4] = mine[...]
    for copy in copies:
        copy.wait()


def exchange(cells, frac, species, counts):
    atoms = cells.shape[-1]
    return pl.pallas_call(
        functools.partial(exchange_kernel, counts),
        out_shape=jax.ShapeDtypeStruct((9, 8, atoms), F32),
        in_specs=[pl.BlockSpec(memory_space=VMEM)] * 3,
        out_specs=pl.BlockSpec(memory_space=VMEM),
        scratch_shapes=[
            VMEM((8, atoms), F32),
            pltpu.SemaphoreType.DMA((8,)),
            pltpu.SemaphoreType.DMA((8,)),
        ],
        compiler_params=pltpu.CompilerParams(collective_id=0, has_side_effects=True),
        name="exchange",
    )(cells, frac, species)


def half_tanh_silu(x):
    half = 0.5 * x
    return half + half * jnp.tanh(half)


def message_kernel(
    planes,
    ext_ref,
    nbr_ref,
    count_ref,
    embed_ref,
    win_ref,
    wout_ref,
    mix_ref,
    prod_ref,
    read_ref,
    charge_ref,
    out_ref,
    placed,
    found,
    weight,
    basis,
    onehot,
    radial,
    state,
    total,
):
    atoms = ext_ref.shape[-1]
    slots = nbr_ref.shape[0]
    tiles = atoms // 128
    channels = embed_ref.shape[1]
    for b in range(9):
        row = lax.broadcasted_iota(jnp.int32, (8, atoms), 0)
        shift = jnp.where(
            row == 0, planes[0] * (b // 3 - 1.0), jnp.where(row == 1, planes[1] * (b % 3 - 1.0), 0.0)
        )
        placed[b] = ext_ref[b] + shift

    def gather(t, carry):
        rows = pl.ds(pl.multiple_of((t // tiles) * 8, 8), 8)
        lanes = pl.ds(pl.multiple_of((t % tiles) * 128, 128), 128)
        index = nbr_ref[rows, lanes]
        low = index & 127
        high = index >> 7
        values = [jnp.zeros((8, 128), F32) for _ in range(4)]
        for r in range(ROW_LOW, ROW_HIGH + 1):
            here = high == r
            piece = slice((r % tiles) * 128, (r % tiles) * 128 + 128)
            for c in range(4):
                line = jnp.broadcast_to(placed[r // tiles, c : c + 1, piece], (8, 128))
                picked = jnp.take_along_axis(line, low, axis=1)
                values[c] = jnp.where(here, picked, values[c])
        for c in range(4):
            found[c, rows, lanes] = values[c]
        return carry

    lax.fori_loop(0, (slots // 8) * tiles, gather, 0)

    own = ext_ref[4]
    dx = (found[0] - own[0:1]) * spacing
    dy = (found[1] - own[1:2]) * spacing
    dz = (found[2] - own[2:3]) * spacing
    distance = jnp.sqrt(dx * dx + dy * dy + dz * dz)
    inverse = 1.0 / distance
    ux, uy, uz = dx * inverse, dy * inverse, dz * inverse
    scaled = distance * (1.0 / cutoff)
    scaled_sq = scaled * scaled
    six = scaled_sq * scaled_sq * scaled_sq
    envelope = 1.0 - 28.0 * six + 48.0 * six * scaled - 21.0 * six * scaled_sq
    slot = lax.broadcasted_iota(jnp.int32, (slots, atoms), 0)
    active = (slot < count_ref[...]) & (scaled < 1.0)
    envelope = jnp.where(active, envelope * neighbour_scale, 0.0)
    r3, r5, r15 = math.sqrt(3.0), math.sqrt(5.0), math.sqrt(15.0)
    factors = (
        None,
        r3 * ux,
        r3 * uy,
        r3 * uz,
        r15 * ux * uy,
        r15 * uy * uz,
        0.5 * r5 * (3.0 * uz * uz - 1.0),
        r15 * ux * uz,
        0.5 * r15 * (ux * ux - uy * uy),
    )
    for m, factor in enumerate(factors):
        full = envelope if factor is None else envelope * factor
        for q in range(slots // 8):
            weight[m, q] = full[8 * q : 8 * q + 8]
    theta = (math.pi / cutoff) * distance
    sine = jnp.sin(theta)
    cosine = 2.0 * jnp.cos(theta)
    scale = math.sqrt(2.0 / cutoff) * inverse
    before = jnp.zeros_like(sine)
    species = found[3]
    for n in range(8):
        value = scale * sine
        marks = (species == float(n)).astype(F32)
        for q in range(slots // 8):
            basis[q, 8 * n : 8 * n + 8, :] = value[8 * q : 8 * q + 8]
            onehot[q, 8 * n : 8 * n + 8, :] = marks[8 * q : 8 * q + 8]
        sine, before = cosine * sine - before, sine

    spread_in = (
        lax.broadcasted_iota(jnp.int32, (8, 64), 1) // 8
        == lax.broadcasted_iota(jnp.int32, (8, 64), 0)
    ).astype(BF16)

    def by_slot(matrix_t):
        outputs = matrix_t.shape[0]
        wide = dot(matrix_t.astype(BF16), spread_in)
        full = jnp.concatenate([wide] * 8, axis=0)
        row = lax.broadcasted_iota(jnp.int32, full.shape, 0) // outputs
        column = lax.broadcasted_iota(jnp.int32, full.shape, 1) % 8
        return jnp.where(row == column, full, 0.0).astype(BF16)

    win_wide = by_slot(win_ref[...].astype(F32).T)
    embed_t = embed_ref[...].astype(F32).T
    embed_wide = by_slot(embed_t)
    wout_t = wout_ref[...].astype(F32).T.astype(BF16)
    hidden_size = win_ref.shape[1]
    total[...] = jnp.zeros_like(total)

    def octet(q, carry):
        hidden = dot(win_wide, basis[q].astype(BF16))
        hidden = half_tanh_silu(hidden).astype(BF16)
        state[...] = dot(embed_wide, onehot[q].astype(BF16))
        for k in range(8):
            radial[k] = dot(wout_t, hidden[k * hidden_size : (k + 1) * hidden_size])

        def tile(t, carry):
            lanes = pl.ds(pl.multiple_of((t % tiles) * 128, 128), 128)
            first = pl.multiple_of((t // tiles) * 16, 16)
            sums = [total[m, pl.ds(first, 16), lanes] for m in range(9)]
            for k in range(8):
                near = state[pl.ds(k * channels + first, 16), lanes]
                weighted = [
                    radial[k, pl.ds(l * channels + first, 16), lanes] * near for l in range(3)
                ]
                for m in range(9):
                    line = weight[m, q, k : k + 1, lanes]
                    sums[m] = sums[m] + weighted[DEGREE[m]] * line
            for m in range(9):
                total[m, pl.ds(first, 16), lanes] = sums[m]
            return carry

        lax.fori_loop(0, tiles * (channels // 16), tile, 0)
        return carry

    lax.fori_loop(0, slots // 8, octet, 0)

    invariants = [None, None, None]
    for m in range(9):
        degree = DEGREE[m]
        mix_t = mix_ref[degree].astype(F32).T.astype(BF16)
        mixed = dot(mix_t, total[m].astype(BF16))
        if degree == 0:
            invariants[0] = mixed
        elif invariants[degree] is None:
            invariants[degree] = mixed * mixed
        else:
            invariants[degree] = invariants[degree] + mixed * mixed
    stacked = jnp.concatenate(invariants, axis=0).astype(BF16)
    prod_t = prod_ref[...].astype(F32).T.astype(BF16)
    update = dot(prod_t, stacked)
    update = update / (1.0 + jnp.exp(-update))
    kinds = lax.broadcasted_iota(jnp.int32, (8, atoms), 0).astype(F32)
    own_state = dot(embed_t.astype(BF16), (kinds == own[3:4]).astype(BF16))
    new_state = (own_state + update).astype(BF16)
    rows = jnp.concatenate(
        [read_ref[...], charge_ref[...], jnp.zeros((14, channels), BF16)], axis=0
    )
    out_ref[...] = dot(rows, new_state)[0:8]


def message(ext, nbr_t, count, embed, win, wout, mix, prod, read, charge, planes):
    atoms = ext.shape[-1]
    slots = nbr_t.shape[0]
    channels = embed.shape[1]
    octets = slots // 8
    return pl.pallas_call(
        functools.partial(message_kernel, planes),
        out_shape=jax.ShapeDtypeStruct((8, atoms), F32),
        in_specs=[pl.BlockSpec(memory_space=VMEM)] * 10,
        out_specs=pl.BlockSpec(memory_space=VMEM),
        scratch_shapes=[
            VMEM((9, 8, atoms), F32),
            VMEM((4, slots, atoms), F32),
            VMEM((9, octets, 8, atoms), F32),
            VMEM((octets, 64, atoms), F32),
            VMEM((octets, 64, atoms), F32),
            VMEM((8, 3 * channels, atoms), F32),
            VMEM((8 * channels, atoms), F32),
            VMEM((9, channels, atoms), F32),
        ],
        compiler_params=pltpu.CompilerParams(vmem_limit_bytes=40 << 20),
        name="message",
    )(ext, nbr_t, count, embed, win, wout, mix, prod, read, charge)


def spline_rows(fraction):
    rest = 1.0 - fraction
    square = fraction * fraction
    cube = square * fraction
    return (
        rest * rest * rest * (1.0 / 6.0),
        (3.0 * cube - 6.0 * square + 4.0) * (1.0 / 6.0),
        (-3.0 * cube + 3.0 * square + 3.0 * fraction + 1.0) * (1.0 / 6.0),
        cube * (1.0 / 6.0),
    )


def stencil_rows(rows, first, weights):
    at = lax.broadcasted_iota(jnp.int32, (rows, first.shape[1]), 0) - first
    out = jnp.where(at == 0, weights[0], 0.0)
    for j in range(1, 4):
        out = jnp.where(at == j, weights[j], out)
    return out


def mesh_kernel(
    counts,
    cells_ref,
    frac_ref,
    local_ref,
    zeta_ref,
    x_hi,
    x_lo,
    xt_hi,
    xt_lo,
    y_hi,
    y_lo,
    gain_ref,
    energy_ref,
    potential_ref,
    sums,
    patch32,
    patch,
    received,
    spectrum,
    answer,
    back,
    back32,
    gain,
    product,
    sum_send,
    sum_recv,
    patch_send,
    patch_recv,
    back_send,
    back_recv,
    gain_sem,
):
    domain_count, inner_count = counts
    devices = domain_count * inner_count
    d, i = lax.axis_index("domain"), lax.axis_index("inner")
    me = d * inner_count + i
    atoms = cells_ref.shape[-1]
    per_core = devices // 2

    def device(t):
        return (t // inner_count, lax.rem(t, inner_count))

    def owner(r):
        rest = lax.rem(r, per_core)
        return (rest // 2, lax.rem(rest, 2) * 2 + r // per_core)

    my_plane = d * 2 + i // 2 + per_core * lax.rem(i, 2)
    owns = my_plane < PLANES

    barrier = pltpu.get_barrier_semaphore()

    def greet(k, carry):
        pl.semaphore_signal(
            barrier, inc=1, device_id=device(lax.rem(me + k, devices)), device_id_type=MESH
        )
        return carry

    lax.fori_loop(1, devices, greet, 0)
    gain_copy = pltpu.make_async_copy(
        gain_ref.at[jnp.minimum(my_plane, PLANES - 1) // 2], gain, gain_sem
    )
    gain_copy.start()

    latent = local_ref[1:2, :]
    part = latent[:, 0:128]
    for t in range(1, atoms // 128):
        part = part + latent[:, t * 128 : (t + 1) * 128]
    sums[me] = part

    weights_x = spline_rows(frac_ref[0:1, :])
    weights_y = spline_rows(frac_ref[1:2, :])
    weights_z = spline_rows(frac_ref[2:3, :])
    cell_x, cell_y, cell_z = cells_ref[0:1, :], cells_ref[1:2, :], cells_ref[2:3, :]
    sten_x = stencil_rows(16, cell_x - 1, weights_x)
    rim_x = jnp.where(cell_x == 0, weights_x[0], 0.0)
    sten_z = stencil_rows(40, cell_z - 1 - Z_LOW, weights_z)
    lane = lax.broadcasted_iota(jnp.int32, (128, atoms), 0)
    y_main = split(stencil_rows(128, cell_y, weights_y))
    y_low = split(jnp.where(lane <= 97, stencil_rows(128, cell_y + 65, weights_y), 0.0))
    y_high = split(jnp.where(lane >= 65, stencil_rows(128, cell_y + 32, weights_y), 0.0))
    waves = jnp.dot(zeta_ref[...], sten_z, precision=lax.Precision.HIGHEST)

    pl.semaphore_wait(barrier, devices - 1)

    def sum_copy(k):
        return pltpu.make_async_remote_copy(
            src_ref=sums.at[me],
            dst_ref=sums.at[me],
            send_sem=sum_send.at[k],
            recv_sem=sum_recv.at[k],
            device_id=device(lax.rem(me + k, devices)),
            device_id_type=MESH,
        )

    def sum_start(k, carry):
        sum_copy(k).start()
        return carry

    def sum_wait(k, carry):
        sum_copy(k).wait()
        return carry

    lax.fori_loop(1, devices, sum_start, 0)
    lax.fori_loop(1, devices, sum_wait, 0)
    mean = jnp.sum(jnp.sum(sums[...], axis=0), axis=1, keepdims=True) / (
        atoms * devices
    )
    charge = latent - mean

    charged = waves * charge
    for r in range(PLANES):
        product[16 * r : 16 * r + 16, :] = sten_x * charged[r : r + 1]
    patch32[...] = dot_split(split(product[...]), y_main, dot_nt)
    rim = split(charged * rim_x)
    low = dot_split(rim, y_low, dot_nt)
    high = dot_split(rim, y_high, dot_nt)
    patch32[pl.ds(0, PLANES, 16), :] = patch32[pl.ds(0, PLANES, 16), :] + low[:PLANES]
    patch32[pl.ds(1, PLANES, 16), :] = patch32[pl.ds(1, PLANES, 16), :] + high[:PLANES]
    patch[...] = patch32[...].astype(BF16)

    my_rows = pl.ds(pl.multiple_of(d * 16, 16), 16)
    my_lanes = pl.ds(pl.multiple_of(i * 128, 128), 128)

    def patch_copy(r):
        return pltpu.make_async_remote_copy(
            src_ref=patch.at[pl.ds(pl.multiple_of(r * 16, 16), 16), :],
            dst_ref=received.at[my_rows, my_lanes],
            send_sem=patch_send.at[r],
            recv_sem=patch_recv.at[me],
            device_id=owner(r),
            device_id_type=MESH,
        )

    def patch_start(k, carry):
        r = lax.rem(my_plane + k, PLANES)

        @pl.when(r != my_plane)
        def _():
            patch_copy(r).start()

        return carry

    lax.fori_loop(0, PLANES, patch_start, 0)

    def back_copy(t):
        return pltpu.make_async_remote_copy(
            src_ref=answer.at[
                pl.ds(pl.multiple_of((t // inner_count) * 16, 16), 16),
                pl.ds(pl.multiple_of(lax.rem(t, inner_count) * 128, 128), 128),
            ],
            dst_ref=back.at[pl.ds(pl.multiple_of(my_plane * 16, 16), 16), :],
            send_sem=back_send.at[t],
            recv_sem=back_recv.at[my_plane],
            device_id=device(t),
            device_id_type=MESH,
        )

    gain_copy.wait()

    @pl.when(owns)
    def _():
        mine = pl.ds(pl.multiple_of(my_plane * 16, 16), 16)
        received[my_rows, my_lanes] = patch[mine, :]

        def arrive(k, carry):
            t = lax.rem(me + k, devices)
            pltpu.make_async_remote_copy(
                src_ref=patch.at[pl.ds(0, 16), :],
                dst_ref=received.at[
                    pl.ds(pl.multiple_of((t // inner_count) * 16, 16), 16),
                    pl.ds(pl.multiple_of(lax.rem(t, inner_count) * 128, 128), 128),
                ],
                send_sem=patch_send.at[0],
                recv_sem=patch_recv.at[t],
                device_id=device(t),
                device_id_type=MESH,
            ).wait_recv()
            return carry

        lax.fori_loop(1, devices, arrive, 0)
        grid = received[...]
        along_y = dot(grid, y_hi[...]) + dot(grid, y_lo[...])
        full_y = along_y.shape[1] // 3
        row = lax.rem(lax.broadcasted_iota(jnp.int32, (grid.shape[0], full_y), 0), 16)
        low_rim = jnp.where(row == 0, along_y[:, full_y : 2 * full_y], 0.0)
        high_rim = jnp.where(row == 1, along_y[:, 2 * full_y :], 0.0)
        count_x = grid.shape[0]
        lines = (
            along_y[:, :full_y]
            + pltpu.roll(low_rim, count_x - 1, 0)
            + pltpu.roll(high_rim, count_x - 2, 0)
        )
        spectrum[...] = dot_split((x_hi[...], x_lo[...]), split(lines), dot)
        half = count_x // 2
        top = gain[0:half, :]
        first_row = lax.broadcasted_iota(jnp.int32, (half, full_y), 0) == 0
        bottom = jnp.where(first_row, gain[half : half + 1, :], top)
        filtered = jnp.concatenate([spectrum[0:half] * top, spectrum[half:] * bottom], axis=0)
        lines = dot_split((xt_hi[...], xt_lo[...]), split(filtered), dot)
        wide = jnp.concatenate(
            [
                lines,
                jnp.where(row == 0, pltpu.roll(lines, 1, 0), 0.0),
                jnp.where(row == 1, pltpu.roll(lines, 2, 0), 0.0),
            ],
            axis=1,
        )
        answer[...] = dot_split(split(wide), (y_hi[...], y_lo[...]), dot_nt).astype(BF16)

        def back_start(k, carry):
            back_copy(lax.rem(me + k, devices)).start()
            return carry

        lax.fori_loop(1, devices, back_start, 0)
        back[mine, :] = answer[my_rows, my_lanes]

    def back_arrive(r, carry):
        @pl.when(r != my_plane)
        def _():
            pltpu.make_async_remote_copy(
                src_ref=answer.at[pl.ds(0, 16), pl.ds(0, 128)],
                dst_ref=back.at[pl.ds(pl.multiple_of(r * 16, 16), 16), :],
                send_sem=back_send.at[0],
                recv_sem=back_recv.at[r],
                device_id=owner(r),
                device_id_type=MESH,
            ).wait_recv()

        return carry

    lax.fori_loop(0, PLANES, back_arrive, 0)
    given = back[...]
    at_atoms = dot(given, y_main[0]) + dot(given, y_main[1])
    back32[...] = given.astype(F32)
    product[...] = at_atoms
    at_low = back32[pl.ds(0, PLANES, 16), :].astype(BF16)
    at_high = back32[pl.ds(1, PLANES, 16), :].astype(BF16)
    at_rim = dot(at_low, y_low[0]) + dot(at_low, y_low[1])
    at_rim = at_rim + dot(at_high, y_high[0]) + dot(at_high, y_high[1])
    gathered = jnp.zeros((8, atoms), F32)
    for r in range(PLANES):
        piece = (
            product[16 * r : 16 * r + 8, :] * sten_x[0:8]
            + product[16 * r + 8 : 16 * r + 16, :] * sten_x[8:16]
        )
        gathered = gathered + piece * waves[r : r + 1]
    value = jnp.sum(gathered, axis=0, keepdims=True) + rim_x * jnp.sum(
        at_rim * waves[:PLANES], axis=0, keepdims=True
    )
    potential_ref[...] = value
    energy_ref[...] = local_ref[0:1, :] + 0.5 * charge * value

    def patch_done(r, carry):
        @pl.when(r != my_plane)
        def _():
            patch_copy(r).wait_send()

        return carry

    lax.fori_loop(0, PLANES, patch_done, 0)

    @pl.when(owns)
    def _():
        def back_done(k, carry):
            back_copy(lax.rem(me + k, devices)).wait_send()
            return carry

        lax.fori_loop(1, devices, back_done, 0)


def mesh_potential(cells, frac, local_rows, tables, counts):
    atoms = cells.shape[-1]
    devices = counts[0] * counts[1]
    full_x = counts[0] * 16
    full_y = counts[1] * 64
    lanes = counts[1] * 128
    dma = pltpu.SemaphoreType.DMA
    vmem = pl.BlockSpec(memory_space=VMEM)
    return pl.pallas_call(
        functools.partial(mesh_kernel, counts),
        out_shape=[jax.ShapeDtypeStruct((1, atoms), F32)] * 2,
        in_specs=[vmem] * 10 + [pl.BlockSpec(memory_space=pl.ANY)],
        out_specs=[vmem] * 2,
        scratch_shapes=[
            VMEM((devices, 1, 128), F32),
            VMEM((PLANES * 16, 128), F32),
            VMEM((PLANES * 16, 128), BF16),
            VMEM((full_x, lanes), BF16),
            VMEM((full_x, full_y), F32),
            VMEM((full_x, lanes), BF16),
            VMEM((PLANES * 16, 128), BF16),
            VMEM((PLANES * 16, 128), F32),
            VMEM((full_x // 2 + 8, full_y), F32),
            VMEM((PLANES * 16, atoms), F32),
            dma((devices,)),
            dma((devices,)),
            dma((PLANES,)),
            dma((devices,)),
            dma((devices,)),
            dma((PLANES,)),
            dma,
        ],
        compiler_params=pltpu.CompilerParams(
            collective_id=1, has_side_effects=True, vmem_limit_bytes=48 << 20
        ),
        name="mesh_potential",
    )(
        cells,
        frac,
        local_rows,
        jnp.asarray(tables["zeta"]),
        *[jnp.asarray(part) for name in ("x", "xt", "y") for part in tables[name]],
        jnp.asarray(tables["gain"]),
    )


def local(
    counts,
    atom_cells,
    atom_frac,
    species,
    nbr_index,
    nbr_count,
    embed,
    radial_in,
    radial_out,
    mix_weight,
    product_weight,
    read_weight,
    charge_weight,
):
    planes = (16, 64)
    tables = host_tables(*counts, *planes, 256)
    cells = atom_cells[0, 0]
    frac = atom_frac[0, 0]
    ext = exchange(cells, frac, species[0], counts)
    rows = message(
        ext,
        nbr_index[0, 0].T,
        nbr_count[0],
        embed,
        radial_in[0],
        radial_out[0],
        mix_weight[0],
        product_weight[0],
        read_weight,
        charge_weight[None],
        planes,
    )
    energy, potential = mesh_potential(cells, frac, rows, tables, counts)
    return (energy[None], potential[None])


def solution(mesh):
    counts = (mesh.shape["domain"], mesh.shape["inner"])
    in_specs = (
        P("domain", "inner", None, None),
        P("domain", "inner", None, None),
        P("domain", "inner", None),
        P("domain", "inner", None, None),
        P("domain", "inner", None),
        P(),
        P(),
        P(),
        P(),
        P(),
        P(),
        P(),
    )
    out_specs = (P("domain", "inner", None), P("domain", "inner", None))
    return jax.shard_map(
        functools.partial(local, counts),
        mesh=mesh,
        in_specs=in_specs,
        out_specs=out_specs,
        check_vma=False,
    )
```

time: 616 us -> 103 us (0.17); the launches traced: 608 us -> 102 us
  local copies, waits for them, and re-layouts: 225 us -> 20 us
  matrix products: 140 us -> 0 us
  blocking collectives: 137 us -> 0 us
  Pallas kernels: 0 us -> 81.5 us
  waiting for transfers between devices: 40.3 us -> 0 us
  other arithmetic: 32.3 us -> 0 us
  starting transfers between devices: 30.9 us -> 0 us
    dot_general x34 -> x0, matrix products: 140 us -> none  [the longest x4 17.3 us: transform(): jnp.einsum(einsum_form, spectrum[0], cos_table, precision=highest)]
    gather x3 -> x0, local copies, waits for them, and re-layouts: 118 us -> none  [the longest x2 60 us: edge_basis(): displacement = (placed[:, neighbours] - own_place[:, :, None]) * spacing]
    pallas_call x0 -> x3, Pallas kernels: none -> 81.5 us  [the longest x1 46 us: mesh_potential(): pl.pallas_call(functools.partial(mesh_kernel, counts), out_shape=[jax.Sha...]
    all_to_all x3 -> x0, blocking collectives: 73.7 us -> none  [the longest x1 30.5 us: send_inner(): lax.all_to_all(spectrum, 'inner', split_axis=1, concat_axis=3, tiled=True)]
    psum x1 -> x0, blocking collectives: 63 us -> none  [local(): summed = lax.psum(jnp.sum(latent), ('domain', 'inner'))]
    squeeze x5 -> x0, local copies, waits for them, and re-layouts: 28.3 us -> none  [the longest x1 17.5 us: message_layer(): weighted[:, :, 0]]
    all_to_all x1 -> x0, waiting for transfers between devices: 25.7 us -> none  [send_domain(): lax.all_to_all(spectrum, 'domain', split_axis=1, concat_axis=2, tiled=True)]
    ppermute x12 -> x0, starting transfers between devices: 25 us -> none  [the longest x4 11 us: extended_2(): lax.ppermute(head, axis, [((i + 1) % count, i) for i in range(count)])]
  transfers between devices with their start and end apart: 13 -> 0, of which waited for: 7 -> 0; matrix products, arithmetic and copies ran while one was open for 15% -> 0% of each run, Pallas kernels for 0% -> 0%
where the time goes in v1:
time: 103 us; the launch traced here: 102 us
  Pallas kernels  81.5 us (79%)
  local copies, waits for them, and re-layouts  20 us (19%)
    pallas_call x1, Pallas kernels, mesh_potential(): pl.pallas_call(functools.partial(mesh_kernel, counts), out_shape=[jax.Sha...  46 us
    pallas_call x1, Pallas kernels, message(): pl.pallas_call(functools.partial(message_kernel, planes), out_shape=jax.S...  21.3 us
    unnamed x42, local copies, waits for them, and re-layouts  20 us
    pallas_call x1, Pallas kernels, exchange(): pl.pallas_call(functools.partial(exchange_kernel, counts), out_shape=jax....  14.2 us

profile of v1, /device:TPU:1, one launch (start us, length us, event | category | flops | bytes accessed | tf_op | source)
XLA Modules:
  0.0 102.2 jit_solution(13338805773143603578)
XLA Ops:
  0.6 1.3 %copy.27 = s32[1,1,3,512]{3,2,1,0:T(4,128)} copy(s32[1,1,3,512]{3,1,2,0:T(1,128)} %param.20) | data formatting | bytes 12288
  1.9 1.3 %copy.26 = f32[1,1,3,512]{3,2,1,0:T(4,128)} copy(f32[1,1,3,512]{3,1,2,0:T(1,128)} %param.21) | data formatting | bytes 12288
  3.2 14.2 %exchange.1.ext_ref = f32[9,8,512]{2,1,0:T(8,128)} custom-call(s32[3,512]{1,0:T(4,128)} %bitcast.20, f32[3,512]{1,0:T(4,128)} %bitcast.22, s32[1,512]{1,0:T(1,128)} %bitcast.31), custom_call_target="tpu_custom_call" | custom-call | tf_op jit(solution)/shard_map/exchange/pallas_call | solution.py:172
  17.4 0.0 copy-start.2
  17.4 0.9 copy-done.2
  18.3 0.0 copy-start.7
  18.3 0.9 copy-done.7
  19.2 0.0 copy-start.8
  19.2 0.9 copy-done.8
  20.1 0.0 copy-start.11
  20.1 0.8 copy-done.11
  20.9 0.0 copy-start.12
  20.9 0.8 copy-done.12
  21.7 0.0 copy-start.14
  21.7 0.7 copy-done.14
  22.4 0.0 copy-start.15
  22.4 0.7 copy-done.15
  23.1 0.0 copy-start.16
  23.1 0.7 copy-done.16
  23.8 0.0 copy-start.17
  23.8 0.7 copy-done.17
  24.4 0.0 copy-start.18
  24.4 0.7 copy-done.18
  25.1 21.3 %message.1.local_ref = f32[8,512]{1,0:T(8,128)S(1)} custom-call(f32[9,8,512]{2,1,0:T(8,128)S(1)} %copy-done.2, s32[32,512]{1,0:T(8,128)S(1)} %bitcast.24, s32[1,512]{1,0:T(1,128)S(1)} %bitcast.26, bf16[8,128]{1,0:T(8,128)(2,1)S(1)} %copy-done.15, bf16[8,64]{1,0:T(8,128)(2,1)S(1)} %bitcast.27, bf16[64,384]{1,0:T(8,128)(2,1)S(1)} %bitcast.25, ...), custom_call_target="tpu_custom_call" | custom-call | tf_op jit(solution)/shard_map/message/pallas_call | solution.py:366
  46.4 0.0 copy-start
  46.4 1.1 %copy-done = bf16[512,768]{1,0:T(8,128)(2,1)S(1)} copy-done((bf16[512,768]{1,0:T(8,128)(2,1)S(1)}, bf16[512,768]{1,0:T(8,128)(2,1)}, u32[]{:S(2)}) %copy-start) | copy-done | bytes 786456
  47.6 0.0 copy-start.1
  47.6 1.1 %copy-done.1 = bf16[512,768]{1,0:T(8,128)(2,1)S(1)} copy-done((bf16[512,768]{1,0:T(8,128)(2,1)S(1)}, bf16[512,768]{1,0:T(8,128)(2,1)}, u32[]{:S(2)}) %copy-start.1) | copy-done | bytes 786456
  48.7 0.0 copy-start.3
  48.7 1.0 %copy-done.3 = bf16[512,512]{1,0:T(8,128)(2,1)S(1)} copy-done((bf16[512,512]{1,0:T(8,128)(2,1)S(1)}, bf16[512,512]{1,0:T(8,128)(2,1)}, u32[]{:S(2)}) %copy-start.3) | copy-done | bytes 524312
  49.8 0.0 copy-start.4
  49.8 1.0 %copy-done.4 = bf16[512,512]{1,0:T(8,128)(2,1)S(1)} copy-done((bf16[512,512]{1,0:T(8,128)(2,1)S(1)}, bf16[512,512]{1,0:T(8,128)(2,1)}, u32[]{:S(2)}) %copy-start.4) | copy-done | bytes 524312
  50.8 0.0 copy-start.5
  50.8 1.0 %copy-done.5 = bf16[512,512]{1,0:T(8,128)(2,1)S(1)} copy-done((bf16[512,512]{1,0:T(8,128)(2,1)S(1)}, bf16[512,512]{1,0:T(8,128)(2,1)}, u32[]{:S(2)}) %copy-start.5) | copy-done | bytes 524312
  51.8 0.0 copy-start.6
  51.8 1.0 %copy-done.6 = bf16[512,512]{1,0:T(8,128)(2,1)S(1)} copy-done((bf16[512,512]{1,0:T(8,128)(2,1)S(1)}, bf16[512,512]{1,0:T(8,128)(2,1)}, u32[]{:S(2)}) %copy-start.6) | copy-done | bytes 524312
  52.9 0.0 copy-start.9
  52.9 0.7 copy-done.9
  53.6 0.0 copy-start.10
  53.6 0.7 copy-done.10
  54.3 0.0 copy-start.13
  54.3 0.8 copy-done.13
  55.0 46.0 %mesh_potential.1 = (f32[1,512]{1,0:T(1,128)S(1)}, f32[1,512]{1,0:T(1,128)S(1)}) custom-call(s32[3,512]{1,0:T(4,128)S(1)} %bitcast.21, f32[3,512]{1,0:T(4,128)S(1)} %bitcast.23, f32[8,512]{1,0:T(8,128)S(1)} %message.1.local_ref, f32[72,40]{1,0:T(8,128)S(1)} %copy-done.13, bf16[512,512]{1,0:T(8,128)(2,1)S(1)} %copy-done.6, bf16[512,512]{1,0:T(8,128)(2,1)S(1)} %copy-done.5, ...), custom_call_target="tpu_custom_call" | custom-call | tf_op jit(solution)/shard_map/mesh_potential/pallas_call | solution.py:685
  101.0 0.6 copy.30
  101.6 0.6 copy.31
Async XLA Ops:
  17.4 0.9 copy-start.2
  18.3 0.9 copy-start.7
  19.2 0.9 copy-start.8
  20.1 0.8 copy-start.11
  20.9 0.8 copy-start.12
  21.7 0.7 copy-start.14
  22.4 0.7 copy-start.15
  23.1 0.7 copy-start.16
  23.8 0.7 copy-start.17
  24.4 0.7 copy-start.18
  46.4 1.1 %copy-start = (bf16[512,768]{1,0:T(8,128)(2,1)S(1)}, bf16[512,768]{1,0:T(8,128)(2,1)}, u32[]{:S(2)}) copy-start(bf16[512,768]{1,0:T(8,128)(2,1)} %constant.22.clone.y_lo) | copy-start | bytes 2359300
  47.6 1.1 %copy-start.1 = (bf16[512,768]{1,0:T(8,128)(2,1)S(1)}, bf16[512,768]{1,0:T(8,128)(2,1)}, u32[]{:S(2)}) copy-start(bf16[512,768]{1,0:T(8,128)(2,1)} %constant.21.clone.y_hi) | copy-start | bytes 2359300
  48.7 1.0 %copy-start.3 = (bf16[512,512]{1,0:T(8,128)(2,1)S(1)}, bf16[512,512]{1,0:T(8,128)(2,1)}, u32[]{:S(2)}) copy-start(bf16[512,512]{1,0:T(8,128)(2,1)} %constant.20.clone.xt_lo) | copy-start | bytes 1572868
  49.8 1.0 %copy-start.4 = (bf16[512,512]{1,0:T(8,128)(2,1)S(1)}, bf16[512,512]{1,0:T(8,128)(2,1)}, u32[]{:S(2)}) copy-start(bf16[512,512]{1,0:T(8,128)(2,1)} %constant.19.clone.xt_hi) | copy-start | bytes 1572868
  50.8 1.0 %copy-start.5 = (bf16[512,512]{1,0:T(8,128)(2,1)S(1)}, bf16[512,512]{1,0:T(8,128)(2,1)}, u32[]{:S(2)}) copy-start(bf16[512,512]{1,0:T(8,128)(2,1)} %constant.18.clone.x_lo) | copy-start | bytes 1572868
  51.8 1.0 %copy-start.6 = (bf16[512,512]{1,0:T(8,128)(2,1)S(1)}, bf16[512,512]{1,0:T(8,128)(2,1)}, u32[]{:S(2)}) copy-start(bf16[512,512]{1,0:T(8,128)(2,1)} %constant.17.clone.x_hi) | copy-start | bytes 1572868
  52.9 0.7 copy-start.9
  53.6 0.7 copy-start.10
  54.3 0.8 copy-start.13

commit v2 on v1

v2 whole, which is shorter than its diff:
```python
import functools
import math

import jax
import jax.numpy as jnp
import numpy as np
from jax import lax
from jax.experimental import pallas as pl
from jax.experimental.pallas import tpu as pltpu
from jax.sharding import PartitionSpec as P

MESH = pl.DeviceIdType.MESH
VMEM = pltpu.VMEM
F32 = jnp.float32
BF16 = jnp.bfloat16

spacing = 0.55
cutoff = 5.0
smearing = 0.2
coulomb = 14.399645
neighbour_scale = 0.25

Z_LOW = 111
Z_SPAN = 33
PLANES = 2 * Z_SPAN
ROW_LOW = 504 // 128
ROW_HIGH = 4103 // 128

DEGREE = (0, 1, 1, 1, 2, 2, 2, 2, 2)


def dot(a, b):
    return lax.dot_general(a, b, (((1,), (0,)), ((), ())), preferred_element_type=F32)


def dot_nt(a, b):
    return lax.dot_general(a, b, (((1,), (1,)), ((), ())), preferred_element_type=F32)


def split(x):
    high = x.astype(BF16)
    return high, (x - high.astype(F32)).astype(BF16)


def dot_split(a, b, form):
    return form(a[0], b[0]) + (form(a[0], b[1]) + form(a[1], b[0]))


def basis_rows(length, positions):
    half = length // 2
    k = np.arange(half)
    angle = 2.0 * np.pi * ((k[:, None] * positions[None, :]) % length) / length
    cosine = np.cos(angle)
    sine = np.sin(angle)
    sine[0] = np.cos(np.pi * positions)
    return np.concatenate([cosine, sine], axis=0)


@functools.lru_cache(maxsize=None)
def host_tables(domain_count, inner_count, planes_x, planes_y, depth):
    full_x = planes_x * domain_count
    full_y = planes_y * inner_count
    table_x = basis_rows(full_x, np.arange(full_x))
    table_y = np.zeros((inner_count, 128, 3, full_y))
    for i in range(inner_count):
        all_y = basis_rows(full_y, (planes_y * i - 1 + np.arange(planes_y + 1)) % full_y).T
        table_y[i, : planes_y + 1, 0] = all_y
        table_y[i, 65:98, 1] = all_y[:33]
        table_y[i, 65:97, 2] = all_y[33:]
    table_y = table_y.reshape(inner_count * 128, 3 * full_y)

    def squared_freq(length, count):
        return (np.arange(count) / (length * spacing)) ** 2

    def modulus(length, count):
        return (2.0 + np.cos(2.0 * np.pi * np.arange(count) / length)) ** 2 / 9.0

    def twice(length, count):
        k = np.arange(count)
        return np.where((k == 0) | (k == length // 2), 1.0, 2.0)

    cx, cy, cz = full_x // 2 + 1, full_y // 2 + 1, depth // 2 + 1
    squared = (
        squared_freq(full_x, cx)[:, None, None]
        + squared_freq(full_y, cy)[None, :, None]
        + squared_freq(depth, cz)[None, None, :]
    )
    safe = np.where(squared > 0.0, squared, 1.0)
    moduli = (
        modulus(full_x, cx)[:, None, None]
        * modulus(full_y, cy)[None, :, None]
        * modulus(depth, cz)[None, None, :]
    )
    volume = full_x * full_y * depth * spacing**3
    kernel = (
        coulomb
        * np.exp(-2.0 * np.pi**2 * smearing**2 * squared)
        / (np.pi * volume * safe * moduli)
    )
    kernel = np.where(squared > 0.0, kernel, 0.0)
    kernel = kernel * twice(full_x, cx)[:, None, None] * twice(full_y, cy)[None, :, None]
    step = np.arange(Z_SPAN)
    along = np.cos(2.0 * np.pi * np.arange(cz)[:, None] * step[None, :] / depth)
    along = along * twice(depth, cz)[:, None]
    wave = np.cos(np.pi * (2 * np.arange(Z_SPAN)[None, :] + 1) * step[:, None] / (2 * Z_SPAN))
    wave = wave * np.where(step == 0, 1.0, 2.0)[:, None] / Z_SPAN
    gain = np.moveaxis(kernel @ (along @ wave), 2, 0)
    order_y = np.concatenate([np.arange(full_y // 2), [full_y // 2], np.arange(1, full_y // 2)])
    gain = gain[:, :, order_y]
    half = full_x // 2
    padded = np.zeros((Z_SPAN, half + 8, full_y), np.float32)
    padded[:, :half] = gain[:, :half]
    padded[:, half] = gain[:, half]
    plane = np.arange(PLANES)
    angle = (
        np.pi * (2 * (plane // 2)[:, None] + 1) * np.arange(40)[None, :] / (2 * Z_SPAN)
    )
    zeta = np.where(plane[:, None] % 2 == 0, np.cos(angle), np.sin(angle))
    zeta[:, Z_SPAN:] = 0.0
    zeta_full = np.zeros((72, 40), np.float32)
    zeta_full[:PLANES] = zeta
    return dict(
        x=table_x.astype(np.float32),
        xt=np.ascontiguousarray(table_x.T).astype(np.float32),
        y=table_y.astype(np.float32),
        gain=padded,
        zeta=zeta_full,
    )


def half_tanh_silu(x):
    half = 0.5 * x
    return half + half * jnp.tanh(half)


def message_rows(
    planes,
    ext_ref,
    nbr_ref,
    count_ref,
    embed_ref,
    win_ref,
    wout_ref,
    mix_ref,
    prod_ref,
    read_ref,
    charge_ref,
    placed,
    found,
    weight,
    basis,
    onehot,
    radial,
    state,
    total,
):
    atoms = ext_ref.shape[-1]
    slots = nbr_ref.shape[0]
    tiles = atoms // 128
    channels = embed_ref.shape[1]
    for b in range(9):
        row = lax.broadcasted_iota(jnp.int32, (8, atoms), 0)
        shift = jnp.where(
            row == 0, planes[0] * (b // 3 - 1.0), jnp.where(row == 1, planes[1] * (b % 3 - 1.0), 0.0)
        )
        placed[b] = ext_ref[b] + shift

    def gather(t, carry):
        rows = pl.ds(pl.multiple_of((t // tiles) * 8, 8), 8)
        lanes = pl.ds(pl.multiple_of((t % tiles) * 128, 128), 128)
        index = nbr_ref[rows, lanes]
        low = index & 127
        high = index >> 7
        values = [jnp.zeros((8, 128), F32) for _ in range(4)]
        for r in range(ROW_LOW, ROW_HIGH + 1):
            here = high == r
            piece = slice((r % tiles) * 128, (r % tiles) * 128 + 128)
            for c in range(4):
                line = jnp.broadcast_to(placed[r // tiles, c : c + 1, piece], (8, 128))
                picked = jnp.take_along_axis(line, low, axis=1)
                values[c] = jnp.where(here, picked, values[c])
        for c in range(4):
            found[c, rows, lanes] = values[c]
        return carry

    lax.fori_loop(0, (slots // 8) * tiles, gather, 0)

    own = ext_ref[4]
    dx = (found[0] - own[0:1]) * spacing
    dy = (found[1] - own[1:2]) * spacing
    dz = (found[2] - own[2:3]) * spacing
    distance = jnp.sqrt(dx * dx + dy * dy + dz * dz)
    inverse = 1.0 / distance
    ux, uy, uz = dx * inverse, dy * inverse, dz * inverse
    scaled = distance * (1.0 / cutoff)
    scaled_sq = scaled * scaled
    six = scaled_sq * scaled_sq * scaled_sq
    envelope = 1.0 - 28.0 * six + 48.0 * six * scaled - 21.0 * six * scaled_sq
    slot = lax.broadcasted_iota(jnp.int32, (slots, atoms), 0)
    active = (slot < count_ref[...]) & (scaled < 1.0)
    envelope = jnp.where(active, envelope * neighbour_scale, 0.0)
    r3, r5, r15 = math.sqrt(3.0), math.sqrt(5.0), math.sqrt(15.0)
    factors = (
        None,
        r3 * ux,
        r3 * uy,
        r3 * uz,
        r15 * ux * uy,
        r15 * uy * uz,
        0.5 * r5 * (3.0 * uz * uz - 1.0),
        r15 * ux * uz,
        0.5 * r15 * (ux * ux - uy * uy),
    )
    for m, factor in enumerate(factors):
        full = envelope if factor is None else envelope * factor
        for q in range(slots // 8):
            weight[m, q] = full[8 * q : 8 * q + 8]
    theta = (math.pi / cutoff) * distance
    sine = jnp.sin(theta)
    cosine = 2.0 * jnp.cos(theta)
    scale = math.sqrt(2.0 / cutoff) * inverse
    before = jnp.zeros_like(sine)
    species = found[3]
    for n in range(8):
        value = scale * sine
        marks = (species == float(n)).astype(F32)
        for q in range(slots // 8):
            basis[q, 8 * n : 8 * n + 8, :] = value[8 * q : 8 * q + 8]
            onehot[q, 8 * n : 8 * n + 8, :] = marks[8 * q : 8 * q + 8]
        sine, before = cosine * sine - before, sine

    spread_in = (
        lax.broadcasted_iota(jnp.int32, (8, 64), 1) // 8
        == lax.broadcasted_iota(jnp.int32, (8, 64), 0)
    ).astype(BF16)

    def by_slot(matrix_t):
        outputs = matrix_t.shape[0]
        wide = dot(matrix_t.astype(BF16), spread_in)
        full = jnp.concatenate([wide] * 8, axis=0)
        row = lax.broadcasted_iota(jnp.int32, full.shape, 0) // outputs
        column = lax.broadcasted_iota(jnp.int32, full.shape, 1) % 8
        return jnp.where(row == column, full, 0.0).astype(BF16)

    win_wide = by_slot(win_ref[...].astype(F32).T)
    embed_t = embed_ref[...].astype(F32).T
    embed_wide = by_slot(embed_t)
    wout_t = wout_ref[...].astype(F32).T.astype(BF16)
    hidden_size = win_ref.shape[1]
    total[...] = jnp.zeros_like(total)

    def octet(q, carry):
        hidden = dot(win_wide, basis[q].astype(BF16))
        hidden = half_tanh_silu(hidden).astype(BF16)
        state[...] = dot(embed_wide, onehot[q].astype(BF16))
        for k in range(8):
            radial[k] = dot(wout_t, hidden[k * hidden_size : (k + 1) * hidden_size])

        def tile(t, carry):
            lanes = pl.ds(pl.multiple_of((t % tiles) * 128, 128), 128)
            first = pl.multiple_of((t // tiles) * 16, 16)
            sums = [total[m, pl.ds(first, 16), lanes] for m in range(9)]
            for k in range(8):
                near = state[pl.ds(k * channels + first, 16), lanes]
                weighted = [
                    radial[k, pl.ds(l * channels + first, 16), lanes] * near for l in range(3)
                ]
                for m in range(9):
                    line = weight[m, q, k : k + 1, lanes]
                    sums[m] = sums[m] + weighted[DEGREE[m]] * line
            for m in range(9):
                total[m, pl.ds(first, 16), lanes] = sums[m]
            return carry

        lax.fori_loop(0, tiles * (channels // 16), tile, 0)
        return carry

    lax.fori_loop(0, slots // 8, octet, 0)

    invariants = [None, None, None]
    for m in range(9):
        degree = DEGREE[m]
        mix_t = mix_ref[degree].astype(F32).T.astype(BF16)
        mixed = dot(mix_t, total[m].astype(BF16))
        if degree == 0:
            invariants[0] = mixed
        elif invariants[degree] is None:
            invariants[degree] = mixed * mixed
        else:
            invariants[degree] = invariants[degree] + mixed * mixed
    stacked = jnp.concatenate(invariants, axis=0).astype(BF16)
    prod_t = prod_ref[...].astype(F32).T.astype(BF16)
    update = dot(prod_t, stacked)
    update = update / (1.0 + jnp.exp(-update))
    kinds = lax.broadcasted_iota(jnp.int32, (8, atoms), 0).astype(F32)
    own_state = dot(embed_t.astype(BF16), (kinds == own[3:4]).astype(BF16))
    new_state = (own_state + update).astype(BF16)
    rows = jnp.concatenate(
        [read_ref[...], charge_ref[...], jnp.zeros((14, channels), BF16)], axis=0
    )
    return dot(rows, new_state)


def spline_rows(fraction):
    rest = 1.0 - fraction
    square = fraction * fraction
    cube = square * fraction
    return (
        rest * rest * rest * (1.0 / 6.0),
        (3.0 * cube - 6.0 * square + 4.0) * (1.0 / 6.0),
        (-3.0 * cube + 3.0 * square + 3.0 * fraction + 1.0) * (1.0 / 6.0),
        cube * (1.0 / 6.0),
    )


def stencil_rows(rows, first, weights):
    at = lax.broadcasted_iota(jnp.int32, (rows, first.shape[1]), 0) - first
    out = jnp.where(at == 0, weights[0], 0.0)
    for j in range(1, 4):
        out = jnp.where(at == j, weights[j], out)
    return out


def three_parts(x):
    first = x.astype(BF16).astype(F32)
    second = (x - first).astype(BF16).astype(F32)
    third = (x - first - second).astype(BF16).astype(F32)
    return first, second, third


def at_marks(position, parts):
    out = jnp.where(position == 125, parts[0], 0.0)
    out = jnp.where(position == 126, parts[1], out)
    return jnp.where(position == 127, parts[2], out)


WEIGHTS = ("embed", "win", "wout", "mix", "prod", "read", "charge")


def program_kernel(counts, planes, names, *refs):
    ref = dict(zip(names, refs))
    domain_count, inner_count = counts
    devices = domain_count * inner_count
    per_core = devices // 2
    d, i = lax.axis_index("domain"), lax.axis_index("inner")
    me = d * inner_count + i
    at = (d, i)
    slots, atoms = ref["nbr_in"].shape

    def device(t):
        return (t // inner_count, lax.rem(t, inner_count))

    def owner(r):
        rest = lax.rem(r, per_core)
        return (rest // 2, lax.rem(rest, 2) * 2 + r // per_core)

    my_plane = d * 2 + i // 2 + per_core * lax.rem(i, 2)
    owns = my_plane < PLANES

    def rows16(t):
        return pl.ds(pl.multiple_of(t * 16, 16), 16)

    def lanes128(t):
        return pl.ds(pl.multiple_of(t * 128, 128), 128)

    barrier = pltpu.get_barrier_semaphore()

    def greet(k, carry):
        pl.semaphore_signal(
            barrier, inc=1, device_id=device(lax.rem(me + k, devices)), device_id_type=MESH
        )
        return carry

    lax.fori_loop(1, devices, greet, 0)

    def fetch(n, name):
        source = ref[name + "_in"]
        if name == "gain":
            source = source.at[jnp.minimum(my_plane, PLANES - 1) // 2]
        return pltpu.make_async_copy(source, ref[name], ref["fetch_sem"].at[n])

    fetched = ("cells", "frac", "species", "nbr", "count") + WEIGHTS
    fetched = fetched + ("zeta", "y", "x", "xt", "gain")
    fetches = {name: fetch(n, name) for n, name in enumerate(fetched)}
    for name in fetched:
        fetches[name].start()

    moves = [(dx, dy) for dx in (-1, 0, 1) for dy in (-1, 0, 1) if (dx, dy) != (0, 0)]
    mine, ext = ref["mine"], ref["ext"]
    for name in ("cells", "frac", "species"):
        fetches[name].wait()
    cell = [ref["cells"][c] for c in range(3)]
    fraction = [ref["frac"][c] for c in range(3)]
    mine[...] = jnp.zeros_like(mine)
    for c in range(3):
        mine[c : c + 1, :] = cell[c].astype(F32) + fraction[c]
    mine[3:4, :] = ref["species"][0].astype(F32)
    pl.semaphore_wait(barrier, devices - 1)
    copies = []
    for n, (dx, dy) in enumerate(moves):
        copy = pltpu.make_async_remote_copy(
            src_ref=mine,
            dst_ref=ext.at[(1 - dx) * 3 + (1 - dy)],
            send_sem=ref["ext_send"].at[n],
            recv_sem=ref["ext_recv"].at[n],
            device_id=tuple(
                lax.rem(at[a] + counts[a] + (dx, dy)[a], counts[a]) for a in range(2)
            ),
            device_id_type=MESH,
        )
        copy.start()
        copies.append(copy)
    ext[4] = mine[...]

    weights = [spline_rows(f) for f in fraction]
    sten_x = stencil_rows(16, cell[0] - 1, weights[0])
    rim_x = jnp.where(cell[0] == 0, weights[0][0], 0.0)
    sten_z = stencil_rows(40, cell[2] - 1 - Z_LOW, weights[2])
    lane = lax.broadcasted_iota(jnp.int32, (128, atoms), 0)
    y_main = split(stencil_rows(128, cell[1], weights[1]))
    y_low = split(jnp.where(lane <= 97, stencil_rows(128, cell[1] + 65, weights[1]), 0.0))
    y_high = split(jnp.where(lane >= 65, stencil_rows(128, cell[1] + 32, weights[1]), 0.0))
    for n, part in enumerate(y_main + y_low + y_high):
        ref["sten_y"][n] = part
    fetches["zeta"].wait()
    waves = ref["waves"]
    waves[...] = jnp.dot(ref["zeta"][...], sten_z, precision=lax.Precision.HIGHEST)
    sten = ref["sten_x"]
    sten[...] = sten_x
    product, patch32 = ref["product"], ref["patch32"]

    def y_parts(n):
        return ref["sten_y"][2 * n], ref["sten_y"][2 * n + 1]

    def spread(charged):
        for r in range(PLANES):
            product[16 * r : 16 * r + 16, :] = sten[...] * charged[r : r + 1]
        patch32[...] = dot_split(split(product[...]), y_parts(0), dot_nt)
        rim = split(charged * rim_x)
        low = dot_split(rim, y_parts(1), dot_nt)
        high = dot_split(rim, y_parts(2), dot_nt)
        patch32[pl.ds(0, PLANES, 16), :] = patch32[pl.ds(0, PLANES, 16), :] + low[:PLANES]
        patch32[pl.ds(1, PLANES, 16), :] = patch32[pl.ds(1, PLANES, 16), :] + high[:PLANES]

    def to_owners(patch, received, send_sem, recv_sem):
        def start(k, carry):
            r = lax.rem(my_plane + k, PLANES)

            @pl.when(r != my_plane)
            def _():
                pltpu.make_async_remote_copy(
                    src_ref=patch.at[rows16(r), :],
                    dst_ref=received.at[rows16(d), lanes128(i)],
                    send_sem=send_sem,
                    recv_sem=recv_sem,
                    device_id=owner(r),
                    device_id_type=MESH,
                ).start()

            return carry

        lax.fori_loop(0, PLANES, start, 0)

        @pl.when(owns)
        def _():
            pltpu.make_async_copy(
                patch.at[rows16(my_plane), :], received.at[rows16(d), lanes128(i)], recv_sem
            ).start()

    def wait_bytes(buffer, sem):
        pltpu.make_async_copy(buffer, buffer, sem).wait()

    spread(waves[...])
    ref["ones_patch"][...] = patch32[...].astype(BF16)
    to_owners(ref["ones_patch"], ref["ones"], ref["ones_send"], ref["ones_recv"])

    for name in ("nbr", "count") + WEIGHTS:
        fetches[name].wait()
    for copy in copies:
        copy.wait()
    rows = message_rows(
        planes,
        ext,
        ref["nbr"],
        ref["count"],
        *[ref[name] for name in WEIGHTS],
        *[
            ref[name]
            for name in (
                "placed",
                "found",
                "weight",
                "basis",
                "onehot",
                "radial",
                "state",
                "total",
            )
        ],
    )
    energy, latent = rows[0:1], rows[1:2]

    block_mean = jnp.sum(latent, axis=1, keepdims=True) / atoms
    spread(waves[...] * (latent - block_mean))
    position = lax.broadcasted_iota(jnp.int32, (1, 128), 1)
    marks = at_marks(position, three_parts(block_mean))
    patch32[pl.ds(2, PLANES, 16), :] = patch32[pl.ds(2, PLANES, 16), :] + marks
    ref["patch"][...] = patch32[...].astype(BF16)
    to_owners(ref["patch"], ref["received"], ref["patch_send"], ref["patch_recv"])

    for name in ("y", "x", "xt", "gain"):
        fetches[name].wait()
    answer, back = ref["answer"], ref["back"]

    @pl.when(owns)
    def _():
        grid, coefficient = ref["grid"], ref["coefficient"]
        y_table = split(ref["y"][...])
        x_table = split(ref["x"][...])
        xt_table = split(ref["xt"][...])
        wait_bytes(ref["ones"], ref["ones_recv"])
        wait_bytes(ref["received"], ref["patch_recv"])
        tiles = [slice(t * 128, t * 128 + 128) for t in range(inner_count)]
        means = []
        for t in range(inner_count):
            grid[t] = ref["received"][:, tiles[t]].astype(F32)
            marked = grid[t, pl.ds(2, domain_count, 16), :]
            means.append(
                jnp.sum(jnp.where(position >= 125, marked, 0.0), axis=1, keepdims=True)
            )
        mean = jnp.sum(sum(means), axis=0, keepdims=True) / devices
        for t in range(inner_count):
            coefficient[t] = jnp.broadcast_to(means[t] - mean, (domain_count, 128))
            for b in range(domain_count):
                here = slice(16 * b, 16 * b + 16)
                unit = ref["ones"][here, tiles[t]].astype(F32)
                grid[t, here, :] = grid[t, here, :] + unit * coefficient[t, b : b + 1, :]
        whole = jnp.concatenate([grid[t] for t in range(inner_count)], axis=1)
        along_y = dot_split(split(whole), y_table, dot)
        count_x, full_y = along_y.shape[0], along_y.shape[1] // 3
        row = lax.rem(lax.broadcasted_iota(jnp.int32, (count_x, full_y), 0), 16)
        low_rim = jnp.where(row == 0, along_y[:, full_y : 2 * full_y], 0.0)
        high_rim = jnp.where(row == 1, along_y[:, 2 * full_y :], 0.0)
        lines = (
            along_y[:, :full_y]
            + pltpu.roll(low_rim, count_x - 1, 0)
            + pltpu.roll(high_rim, count_x - 2, 0)
        )
        spectrum = dot_split(x_table, split(lines), dot)
        half = count_x // 2
        top = ref["gain"][0:half, :]
        first_row = lax.broadcasted_iota(jnp.int32, (half, full_y), 0) == 0
        bottom = jnp.where(first_row, ref["gain"][half : half + 1, :], top)
        filtered = jnp.concatenate([spectrum[0:half] * top, spectrum[half:] * bottom], axis=0)
        lines = dot_split(xt_table, split(filtered), dot)
        wide = jnp.concatenate(
            [
                lines,
                jnp.where(row == 0, pltpu.roll(lines, 1, 0), 0.0),
                jnp.where(row == 1, pltpu.roll(lines, 2, 0), 0.0),
            ],
            axis=1,
        )
        values = dot_split(split(wide), y_table, dot_nt)
        spot = lax.rem(lax.broadcasted_iota(jnp.int32, (1, values.shape[1]), 1), 128)
        marks = at_marks(spot, three_parts(mean))
        line = lax.rem(lax.broadcasted_iota(jnp.int32, values.shape, 0), 16)
        answer[...] = jnp.where(line == 2, values + marks, values).astype(BF16)

        def back_start(k, carry):
            t = lax.rem(me + k, devices)
            pltpu.make_async_remote_copy(
                src_ref=answer.at[rows16(t // inner_count), lanes128(lax.rem(t, inner_count))],
                dst_ref=back.at[rows16(my_plane), :],
                send_sem=ref["back_send"],
                recv_sem=ref["back_recv"],
                device_id=device(t),
                device_id_type=MESH,
            ).start()
            return carry

        lax.fori_loop(1, devices, back_start, 0)
        pltpu.make_async_copy(
            answer.at[rows16(d), lanes128(i)], back.at[rows16(my_plane), :], ref["back_recv"]
        ).start()

    wait_bytes(back, ref["back_recv"])
    given = back[...]
    main, low, high = y_parts(0), y_parts(1), y_parts(2)
    product[...] = dot(given, main[0]) + dot(given, main[1])
    back32 = patch32
    back32[...] = given.astype(F32)
    mean = jnp.sum(jnp.where(position >= 125, back32[2:3, :], 0.0), axis=1, keepdims=True)
    at_low = back32[pl.ds(0, PLANES, 16), :].astype(BF16)
    at_high = back32[pl.ds(1, PLANES, 16), :].astype(BF16)
    at_rim = dot(at_low, low[0]) + dot(at_low, low[1])
    at_rim = at_rim + dot(at_high, high[0]) + dot(at_high, high[1])
    gathered = jnp.zeros((8, atoms), F32)
    for r in range(PLANES):
        piece = (
            product[16 * r : 16 * r + 8, :] * sten[0:8]
            + product[16 * r + 8 : 16 * r + 16, :] * sten[8:16]
        )
        gathered = gathered + piece * waves[r : r + 1]
    value = jnp.sum(gathered, axis=0, keepdims=True) + rim_x * jnp.sum(
        at_rim * waves[:PLANES], axis=0, keepdims=True
    )
    ref["potential_out"][...] = value
    ref["energy_out"][...] = energy + 0.5 * (latent - mean) * value

    sent = ref["sent"]
    for sem in (ref["ones_send"], ref["patch_send"]):

        @pl.when(owns)
        def _():
            wait_bytes(sent.at[0 : (PLANES - 1) * 16], sem)

        @pl.when(jnp.logical_not(owns))
        def _():
            wait_bytes(sent.at[0 : PLANES * 16], sem)

    @pl.when(owns)
    def _():
        wait_bytes(sent.at[0 : (devices - 1) * 16], ref["back_send"])


def local(
    counts,
    atom_cells,
    atom_frac,
    species,
    nbr_index,
    nbr_count,
    embed,
    radial_in,
    radial_out,
    mix_weight,
    product_weight,
    read_weight,
    charge_weight,
):
    planes = (16, 64)
    devices = counts[0] * counts[1]
    tables = host_tables(*counts, *planes, 256)
    operands = dict(
        cells=atom_cells.transpose(2, 0, 1, 3)[:, 0],
        frac=atom_frac.transpose(2, 0, 1, 3)[:, 0],
        species=species,
        nbr=nbr_index[0, 0].T,
        count=nbr_count[0],
        embed=embed,
        win=radial_in[0],
        wout=radial_out[0],
        mix=mix_weight[0],
        prod=product_weight[0],
        read=read_weight,
        charge=charge_weight[None],
        **{name: jnp.asarray(tables[name]) for name in ("zeta", "y", "x", "xt", "gain")},
    )
    slots, atoms = operands["nbr"].shape
    channels = embed.shape[1]
    octets = slots // 8
    full_x, full_y, lanes = counts[0] * planes[0], counts[1] * planes[1], counts[1] * 128
    dma = pltpu.SemaphoreType.DMA
    scratch = {
        name: VMEM(value.shape[1:] if name == "gain" else value.shape, value.dtype)
        for name, value in operands.items()
    }
    scratch.update(
        mine=VMEM((8, atoms), F32),
        ext=VMEM((9, 8, atoms), F32),
        placed=VMEM((9, 8, atoms), F32),
        found=VMEM((4, slots, atoms), F32),
        weight=VMEM((9, octets, 8, atoms), F32),
        basis=VMEM((octets, 64, atoms), F32),
        onehot=VMEM((octets, 64, atoms), F32),
        radial=VMEM((8, 3 * channels, atoms), F32),
        state=VMEM((8 * channels, atoms), F32),
        total=VMEM((9, channels, atoms), F32),
        sten_x=VMEM((16, atoms), F32),
        sten_y=VMEM((6, 128, atoms), BF16),
        waves=VMEM((72, atoms), F32),
        product=VMEM((PLANES * 16, atoms), F32),
        patch32=VMEM((PLANES * 16, 128), F32),
        ones_patch=VMEM((PLANES * 16, 128), BF16),
        patch=VMEM((PLANES * 16, 128), BF16),
        ones=VMEM((full_x, lanes), BF16),
        received=VMEM((full_x, lanes), BF16),
        grid=VMEM((counts[1], full_x, 128), F32),
        coefficient=VMEM((counts[1], counts[0], 128), F32),
        answer=VMEM((full_x, lanes), BF16),
        back=VMEM((PLANES * 16, 128), BF16),
        sent=VMEM(((devices - 1) * 16, 128), BF16),
        fetch_sem=dma((len(operands),)),
        ext_send=dma((8,)),
        ext_recv=dma((8,)),
        ones_send=dma,
        ones_recv=dma,
        patch_send=dma,
        patch_recv=dma,
        back_send=dma,
        back_recv=dma,
    )
    names = [name + "_in" for name in operands] + ["energy_out", "potential_out"] + list(scratch)
    vmem = pl.BlockSpec(memory_space=VMEM)
    energy, potential = pl.pallas_call(
        functools.partial(program_kernel, counts, planes, names),
        out_shape=[jax.ShapeDtypeStruct((1, atoms), F32)] * 2,
        in_specs=[pl.BlockSpec(memory_space=pl.ANY)] * len(operands),
        out_specs=[vmem] * 2,
        scratch_shapes=list(scratch.values()),
        compiler_params=pltpu.CompilerParams(
            collective_id=0, has_side_effects=True, vmem_limit_bytes=58 << 20
        ),
        name="potential",
    )(*operands.values())
    return (energy[None], potential[None])


def solution(mesh):
    counts = (mesh.shape["domain"], mesh.shape["inner"])
    in_specs = (
        P("domain", "inner", None, None),
        P("domain", "inner", None, None),
        P("domain", "inner", None),
        P("domain", "inner", None, None),
        P("domain", "inner", None),
        P(),
        P(),
        P(),
        P(),
        P(),
        P(),
        P(),
    )
    out_specs = (P("domain", "inner", None), P("domain", "inner", None))
    return jax.shard_map(
        functools.partial(local, counts),
        mesh=mesh,
        in_specs=in_specs,
        out_specs=out_specs,
        check_vma=False,
    )
```

time: 103 us -> 66.6 us (0.65)
  Pallas kernels: 81.5 us -> 63.3 us
  local copies, waits for them, and re-layouts: 20 us -> 2.48 us
    pallas_call x3 -> x1, Pallas kernels: 81.5 us -> 63.3 us  [local(): pl.pallas_call(functools.partial(program_kernel, counts, planes, names),...]
    unnamed x42 -> x2, local copies, waits for them, and re-layouts: 20 us -> 2.48 us
where the time goes in v2:
time: 66.6 us; the launch traced here: 66.4 us
  Pallas kernels  63.3 us (95%)
  local copies, waits for them, and re-layouts  2.48 us (4%)
    pallas_call x1, Pallas kernels, local(): pl.pallas_call(functools.partial(program_kernel, counts, planes, names),...  63.3 us
    unnamed x2, local copies, waits for them, and re-layouts  2.48 us

profile of v2, /device:TPU:1, one launch (start us, length us, event | category | flops | bytes accessed | tf_op | source)
XLA Modules:
  0.0 66.4 jit_solution(10393557394739767934)
XLA Ops:
  0.6 63.3 %potential.1 = (f32[1,512]{1,0:T(1,128)}, f32[1,512]{1,0:T(1,128)}) custom-call(s32[3,1,512]{2,1,0:T(1,128)} %bitcast.17, f32[3,1,512]{2,1,0:T(1,128)} %bitcast.18, s32[1,1,512]{2,1,0:T(1,128)} %refs_2_.1, s32[32,512]{1,0:T(8,128)} %bitcast.15, s32[1,512]{1,0:T(1,128)} %bitcast.19, bf16[8,128]{1,0:T(8,128)(2,1)} %refs_5_.1, bf16[8,64]{1,0:T(8,128)(2,1)} %bitcast.20, ...), custom_call_target="tpu_custom_call" | custom-call | tf_op jit(solution)/shard_map/potential/pallas_call | solution.py:706
  63.9 1.2 %copy.21 = f32[1,1,512]{2,1,0:T(1,128)} copy(f32[1,1,512]{2,1,0:T(1,128)} %bitcast.22) | data formatting | bytes 4096
  65.2 1.2 %copy.22 = f32[1,1,512]{2,1,0:T(1,128)} copy(f32[1,1,512]{2,1,0:T(1,128)} %bitcast.21) | data formatting | bytes 4096

commit v3 on v2

--- a/solution.py
+++ b/solution.py
@@ -44,6 +44,13 @@
 
 def dot_split(a, b, form):
     return form(a[0], b[0]) + (form(a[0], b[1]) + form(a[1], b[0]))
+
+
+def three_parts(x):
+    first = x.astype(BF16).astype(F32)
+    second = (x - first).astype(BF16).astype(F32)
+    third = (x - first - second).astype(BF16).astype(F32)
+    return first, second, third
 
 
 def basis_rows(length, positions):
@@ -67,7 +74,7 @@
         table_y[i, : planes_y + 1, 0] = all_y
         table_y[i, 65:98, 1] = all_y[:33]
         table_y[i, 65:97, 2] = all_y[33:]
-    table_y = table_y.reshape(inner_count * 128, 3 * full_y)
+    table_y = table_y.transpose(2, 0, 1, 3).reshape(3, inner_count * 128, full_y)
 
     def squared_freq(length, count):
         return (np.arange(count) / (length * spacing)) ** 2
@@ -133,31 +140,63 @@
     return half + half * jnp.tanh(half)
 
 
+def shuffle_matrix(atoms):
+    row = lax.broadcasted_iota(jnp.int32, (atoms, atoms), 0)
+    column = lax.broadcasted_iota(jnp.int32, (atoms, atoms), 1)
+    return (column == row // 8 + (row % 8) * (atoms // 8)).astype(F32).astype(BF16)
+
+
+def message_weights(species, embed_ref, win_ref, wout_ref, win_wide, pair, shuffle, own_state):
+    kinds, channels = embed_ref.shape
+    inputs, hidden = win_ref.shape
+    atoms = species.shape[1]
+    spread_in = (
+        lax.broadcasted_iota(jnp.int32, (8, 64), 1) // 8
+        == lax.broadcasted_iota(jnp.int32, (8, 64), 0)
+    ).astype(F32).astype(BF16)
+    wide = dot(win_ref[...].astype(F32).T.astype(BF16), spread_in)
+    full = jnp.concatenate([wide] * 8, axis=0)
+    row = lax.broadcasted_iota(jnp.int32, full.shape, 0) // hidden
+    column = lax.broadcasted_iota(jnp.int32, full.shape, 1) % 8
+    win_wide[...] = jnp.where(row == column, full, 0.0).astype(BF16)
+    embed = embed_ref[...].astype(F32)
+    out = wout_ref[...].astype(F32)
+    for degree in range(3):
+        part = out[:, degree * channels : (degree + 1) * channels]
+        for s in range(kinds):
+            pair[degree, s * hidden : (s + 1) * hidden, :] = (part * embed[s : s + 1]).astype(BF16)
+    shuffle[...] = shuffle_matrix(atoms)
+    kind = lax.broadcasted_iota(jnp.int32, (128, atoms), 0)
+    marks = (kind == species).astype(F32).T.astype(BF16)
+    padded = jnp.concatenate([embed, jnp.zeros((128 - kinds, channels), F32)], axis=0)
+    own_state[...] = dot(shuffle[...], dot(marks, padded.astype(BF16)).astype(BF16))
+
+
 def message_rows(
     planes,
     ext_ref,
     nbr_ref,
     count_ref,
-    embed_ref,
-    win_ref,
-    wout_ref,
     mix_ref,
     prod_ref,
     read_ref,
     charge_ref,
+    win_wide,
+    pair,
+    shuffle,
+    own_state,
     placed,
     found,
     weight,
     basis,
-    onehot,
-    radial,
-    state,
-    total,
+    kinds,
+    moments,
 ):
     atoms = ext_ref.shape[-1]
     slots = nbr_ref.shape[0]
     tiles = atoms // 128
-    channels = embed_ref.shape[1]
+    channels = mix_ref.shape[-1]
+    hidden_size = pair.shape[1] // 8
     for b in range(9):
         row = lax.broadcasted_iota(jnp.int32, (8, atoms), 0)
         shift = jnp.where(
@@ -179,16 +218,28 @@
                 line = jnp.broadcast_to(placed[r // tiles, c : c + 1, piece], (8, 128))
                 picked = jnp.take_along_axis(line, low, axis=1)
                 values[c] = jnp.where(here, picked, values[c])
+        into = pl.ds(pl.multiple_of((t % tiles) * slots + (t // tiles) * 8, 8), 8)
         for c in range(4):
-            found[c, rows, lanes] = values[c]
+            found[c, into, :] = values[c]
         return carry
 
     lax.fori_loop(0, (slots // 8) * tiles, gather, 0)
 
     own = ext_ref[4]
-    dx = (found[0] - own[0:1]) * spacing
-    dy = (found[1] - own[1:2]) * spacing
-    dz = (found[2] - own[2:3]) * spacing
+    slot = lax.broadcasted_iota(jnp.int32, (slots, 128), 0)
+    parts = []
+    for c in range(4):
+        pieces = []
+        for j in range(tiles):
+            lanes = slice(j * 128, j * 128 + 128)
+            value = found[c, slots * j : slots * j + slots, :]
+            if c < 3:
+                value = (value - own[c : c + 1, lanes]) * spacing
+            else:
+                value = jnp.where(slot < count_ref[0:1, lanes], value, 8.0)
+            pieces.append(value)
+        parts.append(jnp.concatenate(pieces, axis=0).T)
+    dx, dy, dz, species = parts
     distance = jnp.sqrt(dx * dx + dy * dy + dz * dz)
     inverse = 1.0 / distance
     ux, uy, uz = dx * inverse, dy * inverse, dz * inverse
@@ -196,9 +247,7 @@
     scaled_sq = scaled * scaled
     six = scaled_sq * scaled_sq * scaled_sq
     envelope = 1.0 - 28.0 * six + 48.0 * six * scaled - 21.0 * six * scaled_sq
-    slot = lax.broadcasted_iota(jnp.int32, (slots, atoms), 0)
-    active = (slot < count_ref[...]) & (scaled < 1.0)
-    envelope = jnp.where(active, envelope * neighbour_scale, 0.0)
+    envelope = jnp.where(scaled < 1.0, envelope * neighbour_scale, 0.0)
     r3, r5, r15 = math.sqrt(3.0), math.sqrt(5.0), math.sqrt(15.0)
     factors = (
         None,
@@ -211,94 +260,77 @@
         r15 * ux * uz,
         0.5 * r15 * (ux * ux - uy * uy),
     )
+    octets = 8
+
+    def put(target, first, value):
+        for o in range(octets):
+            target[o, first : first + 8, 0:128] = value[8 * o : 8 * o + 8]
+            target[o, first : first + 8, 128:256] = value[64 + 8 * o : 64 + 8 * o + 8]
+
     for m, factor in enumerate(factors):
-        full = envelope if factor is None else envelope * factor
-        for q in range(slots // 8):
-            weight[m, q] = full[8 * q : 8 * q + 8]
+        put(weight, 8 * m, envelope if factor is None else envelope * factor)
+    put(kinds, 0, species)
     theta = (math.pi / cutoff) * distance
     sine = jnp.sin(theta)
     cosine = 2.0 * jnp.cos(theta)
     scale = math.sqrt(2.0 / cutoff) * inverse
     before = jnp.zeros_like(sine)
-    species = found[3]
     for n in range(8):
-        value = scale * sine
-        marks = (species == float(n)).astype(F32)
-        for q in range(slots // 8):
-            basis[q, 8 * n : 8 * n + 8, :] = value[8 * q : 8 * q + 8]
-            onehot[q, 8 * n : 8 * n + 8, :] = marks[8 * q : 8 * q + 8]
+        put(basis, 8 * n, scale * sine)
         sine, before = cosine * sine - before, sine
 
-    spread_in = (
-        lax.broadcasted_iota(jnp.int32, (8, 64), 1) // 8
-        == lax.broadcasted_iota(jnp.int32, (8, 64), 0)
-    ).astype(BF16)
-
-    def by_slot(matrix_t):
-        outputs = matrix_t.shape[0]
-        wide = dot(matrix_t.astype(BF16), spread_in)
-        full = jnp.concatenate([wide] * 8, axis=0)
-        row = lax.broadcasted_iota(jnp.int32, full.shape, 0) // outputs
-        column = lax.broadcasted_iota(jnp.int32, full.shape, 1) % 8
-        return jnp.where(row == column, full, 0.0).astype(BF16)
-
-    win_wide = by_slot(win_ref[...].astype(F32).T)
-    embed_t = embed_ref[...].astype(F32).T
-    embed_wide = by_slot(embed_t)
-    wout_t = wout_ref[...].astype(F32).T.astype(BF16)
-    hidden_size = win_ref.shape[1]
-    total[...] = jnp.zeros_like(total)
-
-    def octet(q, carry):
-        hidden = dot(win_wide, basis[q].astype(BF16))
+    lane = lax.broadcasted_iota(jnp.int32, (8, 256), 1)
+    element = lax.broadcasted_iota(jnp.int32, (8, 256), 0)
+    mine = ((lane % 128) // slots) * 2 + lane // 128 == element
+
+    def octet(o, carry):
+        hidden = dot(win_wide[...], basis[o].astype(BF16))
         hidden = half_tanh_silu(hidden).astype(BF16)
-        state[...] = dot(embed_wide, onehot[q].astype(BF16))
-        for k in range(8):
-            radial[k] = dot(wout_t, hidden[k * hidden_size : (k + 1) * hidden_size])
-
-        def tile(t, carry):
-            lanes = pl.ds(pl.multiple_of((t % tiles) * 128, 128), 128)
-            first = pl.multiple_of((t // tiles) * 16, 16)
-            sums = [total[m, pl.ds(first, 16), lanes] for m in range(9)]
-            for k in range(8):
-                near = state[pl.ds(k * channels + first, 16), lanes]
-                weighted = [
-                    radial[k, pl.ds(l * channels + first, 16), lanes] * near for l in range(3)
+        for first in range(0, 8, 2):
+            sums = []
+            for i in (first, first + 1):
+                near = hidden[i * hidden_size : (i + 1) * hidden_size]
+                kind = kinds[o, i : i + 1, :]
+                by_kind = []
+                for s in range(8):
+                    mark = jnp.broadcast_to((kind == float(s)).astype(F32), (hidden_size, 256))
+                    by_kind.append(near * mark.astype(BF16))
+                left = [
+                    jnp.where(mine, jnp.broadcast_to(weight[o, 8 * m + i : 8 * m + i + 1, :], (8, 256)), 0.0)
+                    for m in range(9)
                 ]
-                for m in range(9):
-                    line = weight[m, q, k : k + 1, lanes]
-                    sums[m] = sums[m] + weighted[DEGREE[m]] * line
+                left = jnp.concatenate(left, axis=0).astype(BF16)
+                sums.append(dot_nt(left, jnp.concatenate(by_kind, axis=0)))
+            into = pl.ds(pl.multiple_of(64 * o + 8 * first, 16), 16)
             for m in range(9):
-                total[m, pl.ds(first, 16), lanes] = sums[m]
-            return carry
-
-        lax.fori_loop(0, tiles * (channels // 16), tile, 0)
+                both = jnp.concatenate([part[8 * m : 8 * m + 8] for part in sums], axis=0)
+                moments[m, into, :] = both.astype(BF16)
         return carry
 
-    lax.fori_loop(0, slots // 8, octet, 0)
+    lax.fori_loop(0, octets, octet, 0)
 
     invariants = [None, None, None]
     for m in range(9):
         degree = DEGREE[m]
-        mix_t = mix_ref[degree].astype(F32).T.astype(BF16)
-        mixed = dot(mix_t, total[m].astype(BF16))
+        aggregate = dot(moments[m], pair[degree]).astype(BF16)
+        mixed = dot(aggregate, mix_ref[degree])
         if degree == 0:
             invariants[0] = mixed
         elif invariants[degree] is None:
             invariants[degree] = mixed * mixed
         else:
             invariants[degree] = invariants[degree] + mixed * mixed
-    stacked = jnp.concatenate(invariants, axis=0).astype(BF16)
-    prod_t = prod_ref[...].astype(F32).T.astype(BF16)
-    update = dot(prod_t, stacked)
+    stacked = jnp.concatenate(invariants, axis=1).astype(BF16)
+    update = dot(stacked, prod_ref[...])
     update = update / (1.0 + jnp.exp(-update))
-    kinds = lax.broadcasted_iota(jnp.int32, (8, atoms), 0).astype(F32)
-    own_state = dot(embed_t.astype(BF16), (kinds == own[3:4]).astype(BF16))
-    new_state = (own_state + update).astype(BF16)
-    rows = jnp.concatenate(
+    new_state = (own_state[...] + update).astype(BF16)
+    readout = jnp.concatenate(
         [read_ref[...], charge_ref[...], jnp.zeros((14, channels), BF16)], axis=0
     )
-    return dot(rows, new_state)
+    shuffled = dot_nt(readout, new_state)[0:2]
+    stack = jnp.concatenate(three_parts(shuffled) + (jnp.zeros((10, atoms), F32),), axis=0)
+    ordered = dot(stack.astype(BF16), shuffle[...])
+    return ordered[0:2] + ordered[2:4] + ordered[4:6]
 
 
 def spline_rows(fraction):
@@ -319,13 +351,6 @@
     for j in range(1, 4):
         out = jnp.where(at == j, weights[j], out)
     return out
-
-
-def three_parts(x):
-    first = x.astype(BF16).astype(F32)
-    second = (x - first).astype(BF16).astype(F32)
-    third = (x - first - second).astype(BF16).astype(F32)
-    return first, second, third
 
 
 def at_marks(position, parts):
@@ -395,21 +420,6 @@
     for c in range(3):
         mine[c : c + 1, :] = cell[c].astype(F32) + fraction[c]
     mine[3:4, :] = ref["species"][0].astype(F32)
-    pl.semaphore_wait(barrier, devices - 1)
-    copies = []
-    for n, (dx, dy) in enumerate(moves):
-        copy = pltpu.make_async_remote_copy(
-            src_ref=mine,
-            dst_ref=ext.at[(1 - dx) * 3 + (1 - dy)],
-            send_sem=ref["ext_send"].at[n],
-            recv_sem=ref["ext_recv"].at[n],
-            device_id=tuple(
-                lax.rem(at[a] + counts[a] + (dx, dy)[a], counts[a]) for a in range(2)
-            ),
-            device_id_type=MESH,
-        )
-        copy.start()
-        copies.append(copy)
     ext[4] = mine[...]
 
     weights = [spline_rows(f) for f in fraction]
@@ -472,29 +482,59 @@
 
     spread(waves[...])
     ref["ones_patch"][...] = patch32[...].astype(BF16)
-    to_owners(ref["ones_patch"], ref["ones"], ref["ones_send"], ref["ones_recv"])
+    for name, source in (("x", "x"), ("xt", "xt"), ("y", "y")):
+        fetches[source].wait()
+        for n, part in enumerate(split(ref[source][...])):
+            ref[name + "_parts"][n] = part
 
     for name in ("nbr", "count") + WEIGHTS:
         fetches[name].wait()
+    message_weights(
+        ref["species"][0],
+        *[ref[name] for name in ("embed", "win", "wout", "win_wide", "pair", "shuffle", "own_state")],
+    )
+
+    pl.semaphore_wait(barrier, devices - 1)
+    copies = []
+    for n, (dx, dy) in enumerate(moves):
+        copy = pltpu.make_async_remote_copy(
+            src_ref=mine,
+            dst_ref=ext.at[(1 - dx) * 3 + (1 - dy)],
+            send_sem=ref["ext_send"].at[n],
+            recv_sem=ref["ext_recv"].at[n],
+            device_id=tuple(
+                lax.rem(at[a] + counts[a] + (dx, dy)[a], counts[a]) for a in range(2)
+            ),
+            device_id_type=MESH,
+        )
+        copy.start()
+        copies.append(copy)
+    to_owners(ref["ones_patch"], ref["ones"], ref["ones_send"], ref["ones_recv"])
+
     for copy in copies:
         copy.wait()
     rows = message_rows(
         planes,
         ext,
-        ref["nbr"],
-        ref["count"],
-        *[ref[name] for name in WEIGHTS],
         *[
             ref[name]
             for name in (
+                "nbr",
+                "count",
+                "mix",
+                "prod",
+                "read",
+                "charge",
+                "win_wide",
+                "pair",
+                "shuffle",
+                "own_state",
                 "placed",
                 "found",
                 "weight",
                 "basis",
-                "onehot",
-                "radial",
-                "state",
-                "total",
+                "kinds",
+                "moments",
             )
         ],
     )
@@ -508,16 +548,24 @@
     ref["patch"][...] = patch32[...].astype(BF16)
     to_owners(ref["patch"], ref["received"], ref["patch_send"], ref["patch_recv"])
 
-    for name in ("y", "x", "xt", "gain"):
-        fetches[name].wait()
+    fetches["gain"].wait()
     answer, back = ref["answer"], ref["back"]
 
     @pl.when(owns)
     def _():
         grid, coefficient = ref["grid"], ref["coefficient"]
-        y_table = split(ref["y"][...])
-        x_table = split(ref["x"][...])
-        xt_table = split(ref["xt"][...])
+        x_table = ref["x_parts"][0], ref["x_parts"][1]
+        xt_table = ref["xt_parts"][0], ref["xt_parts"][1]
+
+        def y_table(part):
+            return ref["y_parts"][0, part], ref["y_parts"][1, part]
+
+        def whole_rows(rows):
+            return jnp.concatenate([grid[t, rows, :] for t in range(inner_count)], axis=1)
+
+        def every16(first):
+            return pl.ds(first, domain_count, 16)
+
         wait_bytes(ref["ones"], ref["ones_recv"])
         wait_bytes(ref["received"], ref["patch_recv"])
         tiles = [slice(t * 128, t * 128 + 128) for t in range(inner_count)]
@@ -535,37 +583,40 @@
                 here = slice(16 * b, 16 * b + 16)
                 unit = ref["ones"][here, tiles[t]].astype(F32)
                 grid[t, here, :] = grid[t, here, :] + unit * coefficient[t, b : b + 1, :]
-        whole = jnp.concatenate([grid[t] for t in range(inner_count)], axis=1)
-        along_y = dot_split(split(whole), y_table, dot)
-        count_x, full_y = along_y.shape[0], along_y.shape[1] // 3
-        row = lax.rem(lax.broadcasted_iota(jnp.int32, (count_x, full_y), 0), 16)
-        low_rim = jnp.where(row == 0, along_y[:, full_y : 2 * full_y], 0.0)
-        high_rim = jnp.where(row == 1, along_y[:, 2 * full_y :], 0.0)
-        lines = (
-            along_y[:, :full_y]
-            + pltpu.roll(low_rim, count_x - 1, 0)
-            + pltpu.roll(high_rim, count_x - 2, 0)
-        )
+        along_y = dot_split(split(whole_rows(slice(None))), y_table(0), dot)
+        rim = dot_split(split(whole_rows(every16(0))), y_table(1), dot)
+        rim = rim + dot_split(split(whole_rows(every16(1))), y_table(2), dot)
+        rim = pltpu.roll(rim, domain_count - 1, 0)
+        lines_ref = ref["lines"]
+        full_y = along_y.shape[1]
+        columns = [slice(t * 128, t * 128 + 128) for t in range(full_y // 128)]
+        for t, column in enumerate(columns):
+            lines_ref[t] = along_y[:, column]
+            lines_ref[t, every16(15), :] = lines_ref[t, every16(15), :] + rim[:, column]
+        lines = jnp.concatenate([lines_ref[t] for t in range(len(columns))], axis=1)
         spectrum = dot_split(x_table, split(lines), dot)
-        half = count_x // 2
+        half = lines.shape[0] // 2
         top = ref["gain"][0:half, :]
         first_row = lax.broadcasted_iota(jnp.int32, (half, full_y), 0) == 0
         bottom = jnp.where(first_row, ref["gain"][half : half + 1, :], top)
         filtered = jnp.concatenate([spectrum[0:half] * top, spectrum[half:] * bottom], axis=0)
         lines = dot_split(xt_table, split(filtered), dot)
-        wide = jnp.concatenate(
-            [
-                lines,
-                jnp.where(row == 0, pltpu.roll(lines, 1, 0), 0.0),
-                jnp.where(row == 1, pltpu.roll(lines, 2, 0), 0.0),
-            ],
-            axis=1,
+        for t, column in enumerate(columns):
+            lines_ref[t] = lines[:, column]
+        rim = jnp.concatenate(
+            [lines_ref[t, every16(15), :] for t in range(len(columns))], axis=1
         )
-        values = dot_split(split(wide), y_table, dot_nt)
-        spot = lax.rem(lax.broadcasted_iota(jnp.int32, (1, values.shape[1]), 1), 128)
-        marks = at_marks(spot, three_parts(mean))
-        line = lax.rem(lax.broadcasted_iota(jnp.int32, values.shape, 0), 16)
-        answer[...] = jnp.where(line == 2, values + marks, values).astype(BF16)
+        rim = split(pltpu.roll(rim, 1, 0))
+        values = dot_split(split(lines), y_table(0), dot_nt)
+        low_rim = dot_split(rim, y_table(1), dot_nt)
+        high_rim = dot_split(rim, y_table(2), dot_nt)
+        marks = at_marks(position, three_parts(mean))
+        for t in range(inner_count):
+            grid[t] = values[:, tiles[t]]
+            grid[t, every16(0), :] = grid[t, every16(0), :] + low_rim[:, tiles[t]]
+            grid[t, every16(1), :] = grid[t, every16(1), :] + high_rim[:, tiles[t]]
+            grid[t, every16(2), :] = grid[t, every16(2), :] + marks
+            answer[:, tiles[t]] = grid[t].astype(BF16)
 
         def back_start(k, carry):
             t = lax.rem(me + k, devices)
@@ -605,8 +656,8 @@
     value = jnp.sum(gathered, axis=0, keepdims=True) + rim_x * jnp.sum(
         at_rim * waves[:PLANES], axis=0, keepdims=True
     )
-    ref["potential_out"][...] = value
-    ref["energy_out"][...] = energy + 0.5 * (latent - mean) * value
+    ref["out"][0:1] = energy + 0.5 * (latent - mean) * value
+    ref["out"][1:2] = value
 
     sent = ref["sent"]
     for sem in (ref["ones_send"], ref["patch_send"]):
@@ -622,6 +673,11 @@
     @pl.when(owns)
     def _():
         wait_bytes(sent.at[0 : (devices - 1) * 16], ref["back_send"])
+
+
+def part_kernel(both_ref, energy_ref, potential_ref):
+    energy_ref[0] = both_ref[0:1, :]
+    potential_ref[0] = both_ref[1:2, :]
 
 
 def local(
@@ -659,7 +715,7 @@
     )
     slots, atoms = operands["nbr"].shape
     channels = embed.shape[1]
-    octets = slots // 8
+    hidden = radial_in.shape[-1]
     full_x, full_y, lanes = counts[0] * planes[0], counts[1] * planes[1], counts[1] * 128
     dma = pltpu.SemaphoreType.DMA
     scratch = {
@@ -670,13 +726,15 @@
         mine=VMEM((8, atoms), F32),
         ext=VMEM((9, 8, atoms), F32),
         placed=VMEM((9, 8, atoms), F32),
-        found=VMEM((4, slots, atoms), F32),
-        weight=VMEM((9, octets, 8, atoms), F32),
-        basis=VMEM((octets, 64, atoms), F32),
-        onehot=VMEM((octets, 64, atoms), F32),
-        radial=VMEM((8, 3 * channels, atoms), F32),
-        state=VMEM((8 * channels, atoms), F32),
-        total=VMEM((9, channels, atoms), F32),
+        found=VMEM((4, atoms // 128 * slots, 128), F32),
+        weight=VMEM((8, 72, 256), F32),
+        basis=VMEM((8, 64, 256), F32),
+        kinds=VMEM((8, 8, 256), F32),
+        moments=VMEM((9, atoms, 8 * hidden), BF16),
+        win_wide=VMEM((8 * hidden, 64), BF16),
+        pair=VMEM((3, 8 * hidden, channels), BF16),
+        shuffle=VMEM((atoms, atoms), BF16),
+        own_state=VMEM((atoms, channels), F32),
         sten_x=VMEM((16, atoms), F32),
         sten_y=VMEM((6, 128, atoms), BF16),
         waves=VMEM((72, atoms), F32),
@@ -688,6 +746,10 @@
         received=VMEM((full_x, lanes), BF16),
         grid=VMEM((counts[1], full_x, 128), F32),
         coefficient=VMEM((counts[1], counts[0], 128), F32),
+        lines=VMEM((full_y // 128, full_x, 128), F32),
+        x_parts=VMEM((2, full_x, full_x), BF16),
+        xt_parts=VMEM((2, full_x, full_x), BF16),
+        y_parts=VMEM((2, 3, lanes, full_y), BF16),
         answer=VMEM((full_x, lanes), BF16),
         back=VMEM((PLANES * 16, 128), BF16),
         sent=VMEM(((devices - 1) * 16, 128), BF16),
@@ -701,20 +763,28 @@
         back_send=dma,
         back_recv=dma,
     )
-    names = [name + "_in" for name in operands] + ["energy_out", "potential_out"] + list(scratch)
+    names = [name + "_in" for name in operands] + ["out"] + list(scratch)
     vmem = pl.BlockSpec(memory_space=VMEM)
-    energy, potential = pl.pallas_call(
+    both = pl.pallas_call(
         functools.partial(program_kernel, counts, planes, names),
-        out_shape=[jax.ShapeDtypeStruct((1, atoms), F32)] * 2,
+        out_shape=jax.ShapeDtypeStruct((2, atoms), F32),
         in_specs=[pl.BlockSpec(memory_space=pl.ANY)] * len(operands),
-        out_specs=[vmem] * 2,
+        out_specs=vmem,
         scratch_shapes=list(scratch.values()),
         compiler_params=pltpu.CompilerParams(
             collective_id=0, has_side_effects=True, vmem_limit_bytes=58 << 20
         ),
         name="potential",
     )(*operands.values())
-    return (energy[None], potential[None])
+    return tuple(
+        pl.pallas_call(
+            part_kernel,
+            out_shape=[jax.ShapeDtypeStruct((1, 1, atoms), F32)] * 2,
+            in_specs=[vmem],
+            out_specs=[vmem] * 2,
+            name="outputs",
+        )(both)
+    )
 
 
 def solution(mesh):

time: 66.6 us -> 59.1 us (0.89)
  Pallas kernels: 63.3 us -> 58.3 us
  local copies, waits for them, and re-layouts: 2.48 us -> 0 us
    pallas_call x1, Pallas kernels: 63.3 us -> 57.1 us  [local(): pl.pallas_call(functools.partial(program_kernel, counts, planes, names),...]
    unnamed x2 -> x0, local copies, waits for them, and re-layouts: 2.48 us -> none
    pallas_call x0 -> x1, Pallas kernels: none -> 1.27 us  [local(): pl.pallas_call(part_kernel, out_shape=[jax.ShapeDtypeStruct((1, 1, atoms)...]
where the time goes in v3:
time: 59.1 us; the launch traced here: 59 us
  Pallas kernels  58.3 us (99%)
  between operations  0.64 us (1%)
    pallas_call x1, Pallas kernels, local(): pl.pallas_call(functools.partial(program_kernel, counts, planes, names),...  57.1 us
    pallas_call x1, Pallas kernels, local(): pl.pallas_call(part_kernel, out_shape=[jax.ShapeDtypeStruct((1, 1, atoms)...  1.27 us

profile of v3, /device:TPU:1, one launch (start us, length us, event | category | flops | bytes accessed | tf_op | source)
XLA Modules:
  0.0 59.0 jit_solution(14810884515329307879)
XLA Ops:
  0.6 57.1 %potential.1.both_ref = f32[2,512]{1,0:T(2,128)} custom-call(s32[3,1,512]{2,1,0:T(1,128)} %bitcast.15, f32[3,1,512]{2,1,0:T(1,128)} %bitcast.16, s32[1,1,512]{2,1,0:T(1,128)} %refs_2_.1, s32[32,512]{1,0:T(8,128)} %bitcast.13, s32[1,512]{1,0:T(1,128)} %bitcast.17, bf16[8,128]{1,0:T(8,128)(2,1)} %refs_5_.1, bf16[8,64]{1,0:T(8,128)(2,1)} %bitcast.18, ...), custom_call_target="tpu_custom_call" | custom-call | tf_op jit(solution)/shard_map/potential/pallas_call | solution.py:768
  57.7 1.3 %outputs.1 = (f32[1,1,512]{2,1,0:T(1,128)}, f32[1,1,512]{2,1,0:T(1,128)}) custom-call(f32[2,512]{1,0:T(2,128)} %potential.1.both_ref), custom_call_target="tpu_custom_call" | custom-call | tf_op jit(solution)/shard_map/outputs/pallas_call | solution.py:780

commit v4 on v3

--- a/solution.py
+++ b/solution.py
@@ -293,8 +293,8 @@
                 kind = kinds[o, i : i + 1, :]
                 by_kind = []
                 for s in range(8):
-                    mark = jnp.broadcast_to((kind == float(s)).astype(F32), (hidden_size, 256))
-                    by_kind.append(near * mark.astype(BF16))
+                    mark = jnp.broadcast_to((kind == float(s)).astype(F32), (16, 256)).astype(BF16)
+                    by_kind.append(near * jnp.concatenate([mark] * (hidden_size // 16), axis=0))
                 left = [
                     jnp.where(mine, jnp.broadcast_to(weight[o, 8 * m + i : 8 * m + i + 1, :], (8, 256)), 0.0)
                     for m in range(9)
@@ -309,17 +309,15 @@
 
     lax.fori_loop(0, octets, octet, 0)
 
-    invariants = [None, None, None]
-    for m in range(9):
-        degree = DEGREE[m]
-        aggregate = dot(moments[m], pair[degree]).astype(BF16)
+    invariants = []
+    for degree, (first, last) in enumerate(((0, 1), (1, 4), (4, 9))):
+        rows = moments[first:last].reshape((last - first) * atoms, moments.shape[2])
+        aggregate = dot(rows, pair[degree]).astype(BF16)
         mixed = dot(aggregate, mix_ref[degree])
-        if degree == 0:
-            invariants[0] = mixed
-        elif invariants[degree] is None:
-            invariants[degree] = mixed * mixed
-        else:
-            invariants[degree] = invariants[degree] + mixed * mixed
+        if degree > 0:
+            mixed = mixed * mixed
+            mixed = sum(mixed[n * atoms : (n + 1) * atoms] for n in range(last - first))
+        invariants.append(mixed)
     stacked = jnp.concatenate(invariants, axis=1).astype(BF16)
     update = dot(stacked, prod_ref[...])
     update = update / (1.0 + jnp.exp(-update))
@@ -359,6 +357,18 @@
     return jnp.where(position == 127, parts[2], out)
 
 
+def several(first, last, unroll, step):
+    def turn(n, carry):
+        for k in range(unroll):
+            step(first + n * unroll + k)
+        return carry
+
+    turns = (last - first) // unroll
+    lax.fori_loop(0, turns, turn, 0)
+    for k in range(first + turns * unroll, last):
+        step(k)
+
+
 WEIGHTS = ("embed", "win", "wout", "mix", "prod", "read", "charge")
 
 
@@ -390,13 +400,12 @@
 
     barrier = pltpu.get_barrier_semaphore()
 
-    def greet(k, carry):
+    def greet(k):
         pl.semaphore_signal(
             barrier, inc=1, device_id=device(lax.rem(me + k, devices)), device_id_type=MESH
         )
-        return carry
-
-    lax.fori_loop(1, devices, greet, 0)
+
+    several(1, devices, 7, greet)
 
     def fetch(n, name):
         source = ref[name + "_in"]
@@ -453,23 +462,22 @@
         patch32[pl.ds(1, PLANES, 16), :] = patch32[pl.ds(1, PLANES, 16), :] + high[:PLANES]
 
     def to_owners(patch, received, send_sem, recv_sem):
-        def start(k, carry):
+        def start(k):
             r = lax.rem(my_plane + k, PLANES)
-
-            @pl.when(r != my_plane)
-            def _():
-                pltpu.make_async_remote_copy(
-                    src_ref=patch.at[rows16(r), :],
-                    dst_ref=received.at[rows16(d), lanes128(i)],
-                    send_sem=send_sem,
-                    recv_sem=recv_sem,
-                    device_id=owner(r),
-                    device_id_type=MESH,
-                ).start()
-
-            return carry
-
-        lax.fori_loop(0, PLANES, start, 0)
+            pltpu.make_async_remote_copy(
+                src_ref=patch.at[rows16(r), :],
+                dst_ref=received.at[rows16(d), lanes128(i)],
+                send_sem=send_sem,
+                recv_sem=recv_sem,
+                device_id=owner(r),
+                device_id_type=MESH,
+            ).start()
+
+        several(1, PLANES, 5, start)
+
+        @pl.when(jnp.logical_not(owns))
+        def _():
+            start(PLANES)
 
         @pl.when(owns)
         def _():
@@ -618,7 +626,7 @@
             grid[t, every16(2), :] = grid[t, every16(2), :] + marks
             answer[:, tiles[t]] = grid[t].astype(BF16)
 
-        def back_start(k, carry):
+        def back_start(k):
             t = lax.rem(me + k, devices)
             pltpu.make_async_remote_copy(
                 src_ref=answer.at[rows16(t // inner_count), lanes128(lax.rem(t, inner_count))],
@@ -628,9 +636,8 @@
                 device_id=device(t),
                 device_id_type=MESH,
             ).start()
-            return carry
-
-        lax.fori_loop(1, devices, back_start, 0)
+
+        several(1, devices, 7, back_start)
         pltpu.make_async_copy(
             answer.at[rows16(d), lanes128(i)], back.at[rows16(my_plane), :], ref["back_recv"]
         ).start()

time: 59.1 us -> 57.8 us (0.978)
  Pallas kernels: 58.3 us -> 57 us
    pallas_call x1, Pallas kernels: 57.1 us -> 55.8 us  [local(): pl.pallas_call(functools.partial(program_kernel, counts, planes, names),...]
where the time goes in v4:
time: 57.8 us; the launch traced here: 57.7 us
  Pallas kernels  57 us (99%)
  between operations  0.64 us (1%)
    pallas_call x1, Pallas kernels, local(): pl.pallas_call(functools.partial(program_kernel, counts, planes, names),...  55.8 us
    pallas_call x1, Pallas kernels, local(): pl.pallas_call(part_kernel, out_shape=[jax.ShapeDtypeStruct((1, 1, atoms)...  1.27 us

profile of v4, /device:TPU:1, one launch (start us, length us, event | category | flops | bytes accessed | tf_op | source)
XLA Modules:
  0.0 57.7 jit_solution(4188780729591425587)
XLA Ops:
  0.6 55.8 %potential.1.both_ref = f32[2,512]{1,0:T(2,128)} custom-call(s32[3,1,512]{2,1,0:T(1,128)} %bitcast.15, f32[3,1,512]{2,1,0:T(1,128)} %bitcast.16, s32[1,1,512]{2,1,0:T(1,128)} %refs_2_.1, s32[32,512]{1,0:T(8,128)} %bitcast.13, s32[1,512]{1,0:T(1,128)} %bitcast.17, bf16[8,128]{1,0:T(8,128)(2,1)} %refs_5_.1, bf16[8,64]{1,0:T(8,128)(2,1)} %bitcast.18, ...), custom_call_target="tpu_custom_call" | custom-call | tf_op jit(solution)/shard_map/potential/pallas_call | solution.py:775
  56.4 1.3 %outputs.1 = (f32[1,1,512]{2,1,0:T(1,128)}, f32[1,1,512]{2,1,0:T(1,128)}) custom-call(f32[2,512]{1,0:T(2,128)} %potential.1.both_ref), custom_call_target="tpu_custom_call" | custom-call | tf_op jit(solution)/shard_map/outputs/pallas_call | solution.py:787

commit v5 on v4

--- a/solution.py
+++ b/solution.py
@@ -40,6 +40,11 @@
 def split(x):
     high = x.astype(BF16)
     return high, (x - high.astype(F32)).astype(BF16)
+
+
+def dot_left(a, b, form):
+    rounded = a.astype(BF16)
+    return form(rounded, b[0]) + form(rounded, b[1])
 
 
 def dot_split(a, b, form):
@@ -202,7 +207,8 @@
         shift = jnp.where(
             row == 0, planes[0] * (b // 3 - 1.0), jnp.where(row == 1, planes[1] * (b % 3 - 1.0), 0.0)
         )
-        placed[b] = ext_ref[b] + shift
+        block = ext_ref[b] + shift
+        placed[b] = jnp.where(row == 0, block + 64.0 * ext_ref[b, 3:4, :], block)
 
     def gather(t, carry):
         rows = pl.ds(pl.multiple_of((t // tiles) * 8, 8), 8)
@@ -210,17 +216,20 @@
         index = nbr_ref[rows, lanes]
         low = index & 127
         high = index >> 7
-        values = [jnp.zeros((8, 128), F32) for _ in range(4)]
+        values = [jnp.zeros((8, 128), F32) for _ in range(3)]
         for r in range(ROW_LOW, ROW_HIGH + 1):
             here = high == r
             piece = slice((r % tiles) * 128, (r % tiles) * 128 + 128)
-            for c in range(4):
+            for c in range(3):
                 line = jnp.broadcast_to(placed[r // tiles, c : c + 1, piece], (8, 128))
                 picked = jnp.take_along_axis(line, low, axis=1)
                 values[c] = jnp.where(here, picked, values[c])
         into = pl.ds(pl.multiple_of((t % tiles) * slots + (t // tiles) * 8, 8), 8)
-        for c in range(4):
-            found[c, into, :] = values[c]
+        kind = jnp.floor((values[0] + 32.0) * (1.0 / 64.0))
+        found[0, into, :] = values[0] - 64.0 * kind
+        found[1, into, :] = values[1]
+        found[2, into, :] = values[2]
+        found[3, into, :] = kind
         return carry
 
     lax.fori_loop(0, (slots // 8) * tiles, gather, 0)
@@ -591,9 +600,9 @@
                 here = slice(16 * b, 16 * b + 16)
                 unit = ref["ones"][here, tiles[t]].astype(F32)
                 grid[t, here, :] = grid[t, here, :] + unit * coefficient[t, b : b + 1, :]
-        along_y = dot_split(split(whole_rows(slice(None))), y_table(0), dot)
-        rim = dot_split(split(whole_rows(every16(0))), y_table(1), dot)
-        rim = rim + dot_split(split(whole_rows(every16(1))), y_table(2), dot)
+        along_y = dot_left(whole_rows(slice(None)), y_table(0), dot)
+        rim = dot_left(whole_rows(every16(0)), y_table(1), dot)
+        rim = rim + dot_left(whole_rows(every16(1)), y_table(2), dot)
         rim = pltpu.roll(rim, domain_count - 1, 0)
         lines_ref = ref["lines"]
         full_y = along_y.shape[1]
@@ -614,10 +623,10 @@
         rim = jnp.concatenate(
             [lines_ref[t, every16(15), :] for t in range(len(columns))], axis=1
         )
-        rim = split(pltpu.roll(rim, 1, 0))
-        values = dot_split(split(lines), y_table(0), dot_nt)
-        low_rim = dot_split(rim, y_table(1), dot_nt)
-        high_rim = dot_split(rim, y_table(2), dot_nt)
+        rim = pltpu.roll(rim, 1, 0)
+        values = dot_left(lines, y_table(0), dot_nt)
+        low_rim = dot_left(rim, y_table(1), dot_nt)
+        high_rim = dot_left(rim, y_table(2), dot_nt)
         marks = at_marks(position, three_parts(mean))
         for t in range(inner_count):
             grid[t] = values[:, tiles[t]]

time: 57.8 us -> 56.7 us (0.981)
  Pallas kernels: 57 us -> 55.9 us
    pallas_call x1, Pallas kernels: 55.8 us -> 54.6 us  [local(): pl.pallas_call(functools.partial(program_kernel, counts, planes, names),...]
where the time goes in v5:
time: 56.7 us; the launch traced here: 56.5 us
  Pallas kernels  55.9 us (99%)
  between operations  0.64 us (1%)
    pallas_call x1, Pallas kernels, local(): pl.pallas_call(functools.partial(program_kernel, counts, planes, names),...  54.6 us
    pallas_call x1, Pallas kernels, local(): pl.pallas_call(part_kernel, out_shape=[jax.ShapeDtypeStruct((1, 1, atoms)...  1.27 us

profile of v5, /device:TPU:1, one launch (start us, length us, event | category | flops | bytes accessed | tf_op | source)
XLA Modules:
  0.0 56.5 jit_solution(14483773055546804497)
XLA Ops:
  0.6 54.6 %potential.1.both_ref = f32[2,512]{1,0:T(2,128)} custom-call(s32[3,1,512]{2,1,0:T(1,128)} %bitcast.15, f32[3,1,512]{2,1,0:T(1,128)} %bitcast.16, s32[1,1,512]{2,1,0:T(1,128)} %refs_2_.1, s32[32,512]{1,0:T(8,128)} %bitcast.13, s32[1,512]{1,0:T(1,128)} %bitcast.17, bf16[8,128]{1,0:T(8,128)(2,1)} %refs_5_.1, bf16[8,64]{1,0:T(8,128)(2,1)} %bitcast.18, ...), custom_call_target="tpu_custom_call" | custom-call | tf_op jit(solution)/shard_map/potential/pallas_call | solution.py:784
  55.3 1.3 %outputs.1 = (f32[1,1,512]{2,1,0:T(1,128)}, f32[1,1,512]{2,1,0:T(1,128)}) custom-call(f32[2,512]{1,0:T(2,128)} %potential.1.both_ref), custom_call_target="tpu_custom_call" | custom-call | tf_op jit(solution)/shard_map/outputs/pallas_call | solution.py:796

commit v6 on v5

--- a/solution.py
+++ b/solution.py
@@ -232,7 +232,7 @@
         found[3, into, :] = kind
         return carry
 
-    lax.fori_loop(0, (slots // 8) * tiles, gather, 0)
+    lax.fori_loop(0, (slots // 8) * tiles, gather, 0, unroll=2)
 
     own = ext_ref[4]
     slot = lax.broadcasted_iota(jnp.int32, (slots, 128), 0)
@@ -316,7 +316,7 @@
                 moments[m, into, :] = both.astype(BF16)
         return carry
 
-    lax.fori_loop(0, octets, octet, 0)
+    lax.fori_loop(0, octets, octet, 0, unroll=2)
 
     invariants = []
     for degree, (first, last) in enumerate(((0, 1), (1, 4), (4, 9))):
@@ -463,10 +463,10 @@
     def spread(charged):
         for r in range(PLANES):
             product[16 * r : 16 * r + 16, :] = sten[...] * charged[r : r + 1]
-        patch32[...] = dot_split(split(product[...]), y_parts(0), dot_nt)
-        rim = split(charged * rim_x)
-        low = dot_split(rim, y_parts(1), dot_nt)
-        high = dot_split(rim, y_parts(2), dot_nt)
+        patch32[...] = dot_left(product[...], y_parts(0), dot_nt)
+        rim = charged * rim_x
+        low = dot_left(rim, y_parts(1), dot_nt)
+        high = dot_left(rim, y_parts(2), dot_nt)
         patch32[pl.ds(0, PLANES, 16), :] = patch32[pl.ds(0, PLANES, 16), :] + low[:PLANES]
         patch32[pl.ds(1, PLANES, 16), :] = patch32[pl.ds(1, PLANES, 16), :] + high[:PLANES]
 

time: 56.7 us -> 54 us (0.952)
  Pallas kernels: 55.9 us -> 53.2 us
    pallas_call x1, Pallas kernels: 54.6 us -> 52 us  [local(): pl.pallas_call(functools.partial(program_kernel, counts, planes, names),...]
where the time goes in v6:
time: 54 us; the launch traced here: 53.9 us
  Pallas kernels  53.2 us (99%)
  between operations  0.64 us (1%)
    pallas_call x1, Pallas kernels, local(): pl.pallas_call(functools.partial(program_kernel, counts, planes, names),...  52 us
    pallas_call x1, Pallas kernels, local(): pl.pallas_call(part_kernel, out_shape=[jax.ShapeDtypeStruct((1, 1, atoms)...  1.27 us

profile of v6, /device:TPU:1, one launch (start us, length us, event | category | flops | bytes accessed | tf_op | source)
XLA Modules:
  0.0 53.9 jit_solution(4718834342625246551)
XLA Ops:
  0.6 52.0 %potential.1.both_ref = f32[2,512]{1,0:T(2,128)} custom-call(s32[3,1,512]{2,1,0:T(1,128)} %bitcast.15, f32[3,1,512]{2,1,0:T(1,128)} %bitcast.16, s32[1,1,512]{2,1,0:T(1,128)} %refs_2_.1, s32[32,512]{1,0:T(8,128)} %bitcast.13, s32[1,512]{1,0:T(1,128)} %bitcast.17, bf16[8,128]{1,0:T(8,128)(2,1)} %refs_5_.1, bf16[8,64]{1,0:T(8,128)(2,1)} %bitcast.18, ...), custom_call_target="tpu_custom_call" | custom-call | tf_op jit(solution)/shard_map/potential/pallas_call | solution.py:784
  52.6 1.3 %outputs.1 = (f32[1,1,512]{2,1,0:T(1,128)}, f32[1,1,512]{2,1,0:T(1,128)}) custom-call(f32[2,512]{1,0:T(2,128)} %potential.1.both_ref), custom_call_target="tpu_custom_call" | custom-call | tf_op jit(solution)/shard_map/outputs/pallas_call | solution.py:796

commit v7 on v6

--- a/solution.py
+++ b/solution.py
@@ -232,7 +232,7 @@
         found[3, into, :] = kind
         return carry
 
-    lax.fori_loop(0, (slots // 8) * tiles, gather, 0, unroll=2)
+    lax.fori_loop(0, (slots // 8) * tiles, gather, 0, unroll=4)
 
     own = ext_ref[4]
     slot = lax.broadcasted_iota(jnp.int32, (slots, 128), 0)
@@ -316,7 +316,7 @@
                 moments[m, into, :] = both.astype(BF16)
         return carry
 
-    lax.fori_loop(0, octets, octet, 0, unroll=2)
+    lax.fori_loop(0, octets, octet, 0, unroll=4)
 
     invariants = []
     for degree, (first, last) in enumerate(((0, 1), (1, 4), (4, 9))):

time: 54 us -> 53.7 us (level)
  no operation moved by 1% of the time
where the time goes in v7:
time: 53.7 us; the launch traced here: 53.5 us
  Pallas kernels  52.9 us (99%)
  between operations  0.64 us (1%)
    pallas_call x1, Pallas kernels, local(): pl.pallas_call(functools.partial(program_kernel, counts, planes, names),...  51.6 us
    pallas_call x1, Pallas kernels, local(): pl.pallas_call(part_kernel, out_shape=[jax.ShapeDtypeStruct((1, 1, atoms)...  1.27 us

profile of v7, /device:TPU:1, one launch (start us, length us, event | category | flops | bytes accessed | tf_op | source)
XLA Modules:
  0.0 53.5 jit_solution(16713057191739508668)
XLA Ops:
  0.6 51.6 %potential.1.both_ref = f32[2,512]{1,0:T(2,128)} custom-call(s32[3,1,512]{2,1,0:T(1,128)} %bitcast.15, f32[3,1,512]{2,1,0:T(1,128)} %bitcast.16, s32[1,1,512]{2,1,0:T(1,128)} %refs_2_.1, s32[32,512]{1,0:T(8,128)} %bitcast.13, s32[1,512]{1,0:T(1,128)} %bitcast.17, bf16[8,128]{1,0:T(8,128)(2,1)} %refs_5_.1, bf16[8,64]{1,0:T(8,128)(2,1)} %bitcast.18, ...), custom_call_target="tpu_custom_call" | custom-call | tf_op jit(solution)/shard_map/potential/pallas_call | solution.py:784
  52.2 1.3 %outputs.1 = (f32[1,1,512]{2,1,0:T(1,128)}, f32[1,1,512]{2,1,0:T(1,128)}) custom-call(f32[2,512]{1,0:T(2,128)} %potential.1.both_ref), custom_call_target="tpu_custom_call" | custom-call | tf_op jit(solution)/shard_map/outputs/pallas_call | solution.py:796
